TPU v7x, 32 devices: a whole 2x2x4 slice. The times are simulated.
32 devices in a mesh: dp: 8 (over z, x), seq: 4 (over y, core).
Axes of the slice: x: 2, y: 2, z: 4, core: 2. Of those that a mesh axis runs over, the one named last changes fastest.
Arguments:
- tokens: bfloat16 [8, 4096, 768], P('dp', 'seq'), may hold values from -6 to 6
- lengths: int32 [8], P('dp'), may hold values from 512 to 4096, as said below
- cotangent: bfloat16 [8, 4096, 768], P('dp', 'seq'), may hold values from -6 to 6
- norm_gain: float32 [768], replicated, may hold values from 0.5 to 1.5
- w_z: bfloat16 [768, 1536], replicated, may hold values from -0.21875 to 0.21875
- w_xbc: bfloat16 [768, 1792], replicated, may hold values from -0.21875 to 0.21875
- w_dt: bfloat16 [768, 24], replicated, may hold values from -0.21875 to 0.21875
- conv_weight: float32 [4, 1792], replicated, may hold values from -0.5 to 0.5
- conv_bias: float32 [1792], replicated, may hold values from -0.5 to 0.5
- dt_bias: float32 [24], replicated, may hold values from -6 to -3
- a_log: float32 [24], replicated, may hold values from -2.5 to 1
- d_skip: float32 [24], replicated, may hold values from 0.5 to 1.5
- gate_gain: float32 [1536], replicated, may hold values from 0.5 to 1.5
- w_out: bfloat16 [1536, 768], replicated, may hold values from -0.15625 to 0.15625
Outputs:
- block_out: bfloat16 [8, 4096, 768], P('dp', 'seq')
- input_grad: bfloat16 [8, 4096, 768], P('dp', 'seq')
- grad_norm_gain: float32 [768], replicated
- grad_w_z: float32 [768, 1536], replicated
- grad_w_xbc: float32 [768, 1792], replicated
- grad_w_dt: float32 [768, 24], replicated
- grad_conv_weight: float32 [4, 1792], replicated
- grad_conv_bias: float32 [1792], replicated
- grad_dt_bias: float32 [24], replicated
- grad_a_log: float32 [24], replicated
- grad_d_skip: float32 [24], replicated
- grad_gate_gain: float32 [1536], replicated
- grad_w_out: float32 [1536, 768], replicated
Inputs may be any that keep to these rules, and one draw needn't show every extreme that they name: lengths[b] counts the real positions of sequence b, which fill positions 0 to lengths[b] - 1 of its row; the rest is padding. In every draw some sequence fills all 4096 positions.
All inputs are finite; a program needn't handle non-finite values.
Results may differ from a plain program's by a relative error of at most 0.012.
The roundings to bfloat16 on the way count: a program that leaves them out, or rounds other values in their place, can miss the bound.
Values may be sent and summed in bfloat16 or wider, within the bound.
A program may use at most 192 MiB of HBM per device.

v0:
```python
import jax
import jax.numpy as jnp
from jax import lax
from jax.sharding import PartitionSpec as P

HEADS = 24
HEAD_DIM = 64
STATE = 128
CONV = 4
GROUP = 256
INNER = 1536


EPSILON = 1e-05
HIGH = lax.Precision.HIGHEST


def from_behind(shard, axis, by):
    count = lax.axis_size(axis)
    pairs = [(i, i + by) for i in range(count) if 0 <= i + by < count]
    return lax.ppermute(shard, axis, pairs)


def state_scan(values, steps_dt, rates, b_mat, c_mat, plain_intersections):
    total_rows, heads_here, width = values.shape
    group_count = total_rows // GROUP
    state_width = b_mat.shape[1]
    inflow = (steps_dt[:, :, None] * values).reshape(group_count, GROUP, heads_here, width)
    log_rates = jnp.swapaxes(
        (steps_dt * rates[None, :]).reshape(group_count, GROUP, heads_here), 1, 2
    )
    running = jnp.cumsum(log_rates, axis=2)
    causal = jnp.arange(GROUP)[:, None] >= jnp.arange(GROUP)[None, :]
    decays = jnp.exp(jnp.where(causal, running[:, :, :, None] - running[:, :, None, :], -1e30))
    b_groups = b_mat.reshape(group_count, GROUP, state_width)
    c_groups = c_mat.reshape(group_count, GROUP, state_width)
    if plain_intersections:
        intersections = jnp.einsum(
            "ctn,csn->cts",
            c_groups.astype(jnp.bfloat16),
            b_groups.astype(jnp.bfloat16),
            preferred_element_type=jnp.float32,
        )
    else:
        intersections = jnp.einsum("ctn,csn->cts", c_groups, b_groups, precision=HIGH)
    scores = decays * intersections[:, None, :, :]
    within = jnp.einsum("chts,cshp->cthp", scores, inflow, precision=HIGH)
    final_log = running[:, :, -1]
    to_end = jnp.exp(final_log[:, :, None] - running)
    weighted = inflow * jnp.swapaxes(to_end, 1, 2)[:, :, :, None]
    group_state = jnp.einsum("csn,cshp->chpn", b_groups, weighted, precision=HIGH)

    def advance(state_in, carried_item):
        factor, added = carried_item
        return (factor[:, None, None] * state_in + added, state_in)

    zero_state = jnp.zeros((heads_here, width, state_width), jnp.float32)
    unused, starts = lax.scan(advance, zero_state, (jnp.exp(final_log), group_state))
    carried = jnp.einsum("ctn,chpn->cthp", c_groups, starts, precision=HIGH)
    carried = carried * jnp.swapaxes(jnp.exp(running), 1, 2)[:, :, :, None]
    return (within + carried).reshape(total_rows, heads_here, width)


def scan_heads(values, steps_dt, rates, b_and_c):
    return state_scan(values, steps_dt, rates, b_and_c[:, :STATE], b_and_c[:, STATE:], False)


def scan_forward(values, steps_dt, rates, b_and_c):
    return state_scan(values, steps_dt, rates, b_and_c[:, :STATE], b_and_c[:, STATE:], True)


def norm_piece(residual, gain):
    rms = lax.rsqrt(jnp.mean(residual * residual, axis=-1, keepdims=True) + EPSILON)
    return residual * rms * gain[None, :]


def mixer_inputs(extended, dt_raw, conv_weight, conv_bias, dt_bias):
    tok_rows = extended.shape[0] - (CONV - 1)
    conv_out = conv_bias[None, :] + conv_weight[0][None, :] * extended[0:tok_rows]
    for offset in range(1, CONV):
        conv_out = conv_out + conv_weight[offset][None, :] * extended[offset : offset + tok_rows]
    act = jax.nn.silu(conv_out)
    return (act[:, :INNER], act[:, INNER:], jax.nn.softplus(dt_raw + dt_bias[None, :]))


def gate_piece(y_value, gate_pre, gate_gain):
    gated = y_value * jax.nn.silu(gate_pre)
    rms_gate = lax.rsqrt(jnp.mean(gated * gated, axis=-1, keepdims=True) + EPSILON)
    return gated * rms_gate * gate_gain[None, :]


def local(
    tokens,
    lengths,
    cotangent,
    norm_gain,
    w_z,
    w_xbc,
    w_dt,
    conv_weight,
    conv_bias,
    dt_bias,
    a_log,
    d_skip,
    gate_gain,
    w_out,
):
    tok_rows = tokens.shape[1]
    seq_count = lax.axis_size("seq")
    seq_pos = lax.axis_index("seq")
    local_heads = HEADS // seq_count
    head_start = seq_pos * local_heads
    rim_width = CONV - 1
    over_rows = (((0,), (0,)), ((), ()))
    over_cols = (((1,), (1,)), ((), ()))
    residual = tokens[0].astype(jnp.float32)
    normed, norm_back = jax.vjp(norm_piece, residual, norm_gain)
    normed_low = normed.astype(jnp.bfloat16)
    gate_pre = jnp.dot(normed_low, w_z, preferred_element_type=jnp.float32)
    xbc_low = jnp.dot(normed_low, w_xbc, preferred_element_type=jnp.float32).astype(jnp.bfloat16)
    dt_raw = jnp.dot(normed_low, w_dt, preferred_element_type=jnp.float32)
    rim_rows = from_behind(xbc_low[tok_rows - rim_width :], "seq", 1)
    extended = jnp.concatenate([rim_rows, xbc_low], axis=0).astype(jnp.float32)
    (x_value, bc_value, dt_value), input_back = jax.vjp(
        mixer_inputs, extended, dt_raw, conv_weight, conv_bias, dt_bias
    )
    x_low = x_value.astype(jnp.bfloat16).reshape(tok_rows, HEADS, HEAD_DIM)
    bc_low = bc_value.astype(jnp.bfloat16)
    dt_low = dt_value.astype(jnp.bfloat16)
    rate_local = -jnp.exp(lax.dynamic_slice_in_dim(a_log, head_start, local_heads))
    skip_local = lax.dynamic_slice_in_dim(d_skip, head_start, local_heads)
    x_heads, dt_heads = (
        lax.all_to_all(x_low, "seq", split_axis=1, concat_axis=0, tiled=True),
        lax.all_to_all(dt_low, "seq", split_axis=1, concat_axis=0, tiled=True),
    )
    bc_whole = lax.all_gather(bc_low, "seq", axis=0, tiled=True)
    x_heads_f = x_heads.astype(jnp.float32)
    y_scan = scan_forward(
        x_heads_f, dt_heads.astype(jnp.float32), rate_local, bc_whole.astype(jnp.float32)
    )
    y_heads = (y_scan + skip_local[None, :, None] * x_heads_f).astype(jnp.bfloat16)
    y_tokens = lax.all_to_all(y_heads, "seq", split_axis=0, concat_axis=1, tiled=True)
    y_float = y_tokens.reshape(tok_rows, INNER).astype(jnp.float32)
    o_value, gate_back = jax.vjp(gate_piece, y_float, gate_pre, gate_gain)
    o_low = o_value.astype(jnp.bfloat16)
    branch = jnp.dot(o_low, w_out, preferred_element_type=jnp.float32)
    position = seq_pos * tok_rows + jnp.arange(tok_rows, dtype=jnp.int32)
    live = position < lengths[0]
    block_out = (residual + jnp.where(live[:, None], branch, 0.0)).astype(jnp.bfloat16)
    cot_rows = cotangent[0]
    cot_live = jnp.where(live[:, None], cot_rows, jnp.zeros_like(cot_rows))
    grad_w_out = lax.dot_general(o_low, cot_live, over_rows, preferred_element_type=jnp.float32)
    grad_o = lax.dot_general(cot_live, w_out, over_cols, preferred_element_type=jnp.float32)
    grad_y_float, grad_gate_pre, grad_gate_gain = gate_back(grad_o)
    grad_y_low = grad_y_float.astype(jnp.bfloat16).reshape(tok_rows, HEADS, HEAD_DIM)
    grad_gate_low = grad_gate_pre.astype(jnp.bfloat16)
    grad_y_heads = lax.all_to_all(
        grad_y_low, "seq", split_axis=1, concat_axis=0, tiled=True
    ).astype(jnp.float32)
    x_again, dt_again = (
        lax.all_to_all(x_low, "seq", split_axis=1, concat_axis=0, tiled=True),
        lax.all_to_all(dt_low, "seq", split_axis=1, concat_axis=0, tiled=True),
    )
    bc_again = lax.all_gather(bc_low, "seq", axis=0, tiled=True)
    x_saved = x_again.astype(jnp.float32)
    unused_y, back_fn = jax.vjp(
        scan_heads, x_saved, dt_again.astype(jnp.float32), rate_local, bc_again.astype(jnp.float32)
    )
    grad_skip_local = jnp.sum(grad_y_heads * x_saved, axis=(0, 2))
    grad_x_scan, grad_dt_heads, grad_rate, grad_bc_whole = back_fn(grad_y_heads)
    grad_x_heads = (grad_x_scan + skip_local[None, :, None] * grad_y_heads).astype(jnp.bfloat16)
    grad_x_tokens, grad_dt_tokens = (
        lax.all_to_all(grad_x_heads, "seq", split_axis=0, concat_axis=1, tiled=True),
        lax.all_to_all(
            grad_dt_heads.astype(jnp.bfloat16), "seq", split_axis=0, concat_axis=1, tiled=True
        ),
    )
    grad_bc = lax.psum_scatter(
        grad_bc_whole.astype(jnp.bfloat16), "seq", scatter_dimension=0, tiled=True
    ).astype(jnp.float32)
    grad_extended, grad_dt_pre, grad_conv_weight, grad_conv_bias, grad_dt_bias = input_back(
        (
            grad_x_tokens.reshape(tok_rows, INNER).astype(jnp.float32),
            grad_bc,
            grad_dt_tokens.astype(jnp.float32),
        )
    )
    rim_grad = from_behind(grad_extended[:rim_width], "seq", -1)
    grad_own = grad_extended[rim_width:]
    grad_xbc = jnp.concatenate(
        [grad_own[: tok_rows - rim_width], grad_own[tok_rows - rim_width :] + rim_grad], axis=0
    )
    grad_xbc_low = grad_xbc.astype(jnp.bfloat16)
    grad_dt_low = grad_dt_pre.astype(jnp.bfloat16)
    grad_w_z = lax.dot_general(
        normed_low, grad_gate_low, over_rows, preferred_element_type=jnp.float32
    )
    grad_w_xbc = lax.dot_general(
        normed_low, grad_xbc_low, over_rows, preferred_element_type=jnp.float32
    )
    grad_w_dt = lax.dot_general(
        normed_low, grad_dt_low, over_rows, preferred_element_type=jnp.float32
    )
    grad_normed = lax.dot_general(grad_gate_low, w_z, over_cols, preferred_element_type=jnp.float32)
    grad_normed = grad_normed + lax.dot_general(
        grad_xbc_low, w_xbc, over_cols, preferred_element_type=jnp.float32
    )
    grad_normed = grad_normed + lax.dot_general(
        grad_dt_low, w_dt, over_cols, preferred_element_type=jnp.float32
    )
    grad_residual, grad_norm_gain = norm_back(grad_normed)
    input_grad = (cot_rows.astype(jnp.float32) + grad_residual).astype(jnp.bfloat16)
    grad_a_full = lax.dynamic_update_slice_in_dim(
        jnp.zeros((HEADS,), jnp.float32), grad_rate * rate_local, head_start, 0
    )
    grad_skip_full = lax.dynamic_update_slice_in_dim(
        jnp.zeros((HEADS,), jnp.float32), grad_skip_local, head_start, 0
    )
    totals = lax.psum(
        (
            grad_norm_gain,
            grad_w_z,
            grad_w_xbc,
            grad_w_dt,
            grad_conv_weight,
            grad_conv_bias,
            grad_dt_bias,
            grad_a_full,
            grad_skip_full,
            grad_gate_gain,
            grad_w_out,
        ),
        ("dp", "seq"),
    )
    return (
        block_out[None],
        input_grad[None],
        totals[0],
        totals[1],
        totals[2],
        totals[3],
        totals[4],
        totals[5],
        totals[6],
        totals[7],
        totals[8],
        totals[9],
        totals[10],
    )


def solution(mesh):
    return jax.shard_map(
        local,
        mesh=mesh,
        in_specs=(
            P("dp", "seq", None),
            P("dp"),
            P("dp", "seq", None),
            P(),
            P(),
            P(),
            P(),
            P(),
            P(),
            P(),
            P(),
            P(),
            P(),
            P(),
        ),
        out_specs=(
            P("dp", "seq", None),
            P("dp", "seq", None),
            P(),
            P(),
            P(),
            P(),
            P(),
            P(),
            P(),
            P(),
            P(),
            P(),
            P(),
        ),
        check_vma=False,
    )
```

profile of v0, /device:TPU:0, one launch (start us, length us, event | category | flops | bytes accessed | tf_op | source)
XLA Modules:
  0.0 1038.2 jit_solution(10140077979113310308)
XLA Ops:
  9.8 5.1 convolution_convert_fusion
  18.9 6.6 multiply_convert_fusion
  31.6 6.1 all-to-all-start
  41.6 4.6 copy.241
  46.2 5.4 all-to-all-start.1
  58.1 30.6 %all-to-all-done.1 = bf16[1024,24,64]{0,2,1:T(8,128)(2,1)} async-done(((bf16[1024,24,64]{0,2,1:T(8,128)(2,1)}), bf16[1024,24,64]{0,2,1:T(8,128)(2,1)}, u32[]{:S(2)}, u32[]{:S(2)}) %all-to-all-start.1) | async-done | bytes 3145760 | tf_op jit(solution)/shard_map/all_to_all | solution.py:133
  88.7 5.5 convert_bitcast_fusion
  94.2 6.7 copy.242
  101.0 8.4 reshape.297
  109.4 6.6 copy.296
  118.6 11.3 %fusion.33 = f32[16,6,64,128]{3,2,1,0:T(8,128)} fusion(bf16[16,256,128,1]{2,1,3,0:T(8,128)(2,1)S(1)} %bitcast.255, f32[16,256,6,64]{1,0,3,2:T(8,128)} %reshape.297, f32[16,256,6]{1,2,0:T(8,128)S(1)} %get-tuple-element.423, f32[16,256,6]{1,2,0:T(8,128)S(1)} %bitcast.277), kind=kOutput, calls=%fused_computation.83 | convolution fusion | flops 2419064832 | bytes 10682368 | tf_op jit(solution)/shard_map/csn,cshp->chpn/dot_general | solution.py:51
  131.9 27.8 %while.47 = (s32[]{:T(128)}, f32[6,64,128]{2,1,0:T(8,128)S(1)}, f32[16,6,64,128]{3,2,1,0:T(8,128)}, f32[16,6]{1,0:T(8,128)S(1)}, f32[16,6,64,128]{3,2,1,0:T(8,128)}, /*index=5*/s32[]{:T(128)}, s32[]{:T(128)}) while((s32[]{:T(128)}, f32[6,64,128]{2,1,0:T(8,128)S(1)}, f32[16,6,64,128]{3,2,1,0:T(8,128)}, f32[16,6]{1,0:T(8,128)S(1)}, ...), condition=%wide.region_4.5_spmd.clone, body=%wide.region_3.4_spmd.clone.sunk | while | flops 196611 | bytes 983720 | solution.py:58
  162.2 31.4 %fusion.6 = f32[16,6,64,256]{3,2,1,0:T(8,128)S(1)} fusion(f32[16,256,256]{2,1,0:T(8,128)S(1)} %fusion.106, f32[16,6,256]{2,1,0:T(8,128)S(1)} %copy-done.28, pred[256,256]{1,0:T(8,128)(4,1)S(1)} %copy-done.40, f32[16,256,6,64]{1,0,3,2:T(8,128)} %reshape.297, f32[16,256,6]{1,2,0:T(8,128)S(1)} %bitcast.278), kind=kOutput, calls=%fused_computation.19 | convolution fusion | flops 4852285440 | bytes 17039360 | tf_op jit(solution)/shard_map/chts,cshp->cthp/dot_general | solution.py:47
  201.1 9.8 copy.256
  210.9 8.6 reshape.316
  219.4 4.7 all-to-all-start.2
  225.4 35.7 %all-to-all-done.2 = bf16[4,2,196608]{2,1,0:T(2,128)(2,1)} async-done(((bf16[4,2,196608]{2,1,0:T(2,128)(2,1)}), bf16[4,2,196608]{2,1,0:T(2,128)(2,1)}, u32[]{:S(2)}, u32[]{:S(2)}) %all-to-all-start.2) | async-done | bytes 3145760 | tf_op jit(solution)/shard_map/all_to_all | solution.py:142
  261.1 8.2 reshape.317
  269.4 9.1 copy.257
  278.4 8.4 reshape.306
  286.8 9.0 copy.258
  295.8 6.6 copy.259
  302.4 10.0 multiply_reduce_fusion.9
  312.5 6.1 multiply_reduce_fusion.5
  319.8 9.6 fusion.28
  329.4 4.6 copy.261
  334.0 4.7 all-to-all-start.3
  340.8 58.2 %while.48 = (s32[]{:T(128)}, f32[6,64,128]{2,1,0:T(8,128)S(1)}, f32[16,6,64,128]{3,2,1,0:T(8,128)}, f32[16,6,1,1]{1,3,2,0:T(1,128)}, f32[16,6]{1,0:T(8,128)}, /*...) while((s32[]{:T(128)}, f32[6,64,128]{2,1,0:T(8,128)S(1)}, f32[16,6,64,128]{3,2,1,0:T(8,128)}, ...), condition=%wide.region_8.9_spmd.clone, body=%wide.region_7.8_spmd.clone.sunk | while | flops 196611 | bytes 985264 | solution.py:58
  403.3 6.0 copy.262
  409.3 6.0 all_to_all.29
  415.3 7.7 fusion.20
  423.0 28.2 %fusion.9 = (f32[16,6,256]{2,1,0:T(8,128)}, f32[16,6,256]{2,1,0:T(8,128)}, f32[16,256,256]{2,1,0:T(8,128)S(1)}) fusion(f32[16,256,256]{2,1,0:T(8,128)S(1)} %copy-done.17, f32[16,6,256]{2,1,0:T(8,128)S(1)} %copy-done.29, pred[256,256]{1,0:T(8,128)(4,1)S(1)} %copy-done.41, f32[16,256,6,64]{1,0,3,2:T(8,128)} %reshape.297, f32[16,256,6]{1,2,0:T(8,128)S(1)} %bitcast.279, ...), kind=kOutput, calls=%fused_computation.23 | convolution fusion | flops 4888936448 | bytes 18284544 | tf_op jit(solution)/shard_map/transpose(jvp(chts,cshp->cthp))/dot_general | solution.py:47
  451.2 17.5 %fusion.4 = f32[16,6,64,256]{3,2,1,0:T(8,128)} fusion(f32[16,256,256]{2,1,0:T(8,128)S(1)} %copy-done.17, f32[16,6,256]{2,1,0:T(8,128)S(1)} %copy-done.29, pred[256,256]{1,0:T(8,128)(4,1)S(1)} %copy-done.41, bf16[16,256,6,64]{1,0,3,2:T(8,128)(2,1)S(1)} %copy-done.5), kind=kOutput, calls=%fused_computation.16 | convolution fusion | flops 4850712576 | bytes 13795328 | tf_op jit(solution)/shard_map/transpose(jvp(chts,cshp->cthp))/dot_general | solution.py:47
  468.7 5.5 convert_bitcast_fusion.2
  474.2 12.3 %fusion.21 = f32[16,256,128,1]{2,1,3,0:T(8,128)S(1)} fusion(f32[16,6,64,128]{3,2,1,0:T(8,128)S(1)} %copy-done.8, f32[16,256,6]{1,2,0:T(8,128)S(1)} %get-tuple-element.424, bf16[16,256,6,64]{1,0,3,2:T(8,128)(2,1)S(1)} %copy-done.5), kind=kOutput, calls=%fused_computation.44 | convolution fusion | flops 2419064832 | bytes 8486912 | tf_op jit(solution)/shard_map/transpose(jvp(ctn,chpn->cthp))/dot_general | solution.py:59
  486.5 4.9 fusion.24
  491.5 4.9 fusion.108
  501.9 41.0 %while.49 = (s32[]{:T(128)}, f32[6,64,128]{2,1,0:T(8,128)S(1)}, f32[16,6]{1,0:T(8,128)S(1)}, f32[16,6,64,128]{3,2,1,0:T(8,128)}, f32[16,6,64,128]{3,2,1,0:T(8,12...) while((s32[]{:T(128)}, f32[6,64,128]{2,1,0:T(8,128)S(1)}, ...), condition=%wide.region_12.13_spmd.clone, body=%wide.region_10.12_spmd.clone.sunk | while | flops 294910 | bytes 1179932 | solution.py:58
  542.9 16.0 %bitcast_add_fusion.5 = f32[16,256,128]{2,1,0:T(8,128)S(1)} fusion(f32[16,256,128]{2,1,0:T(8,128)} %fusion.108, f32[16,6,64,128]{3,2,1,0:T(8,128)} %get-tuple-element.218, f32[16,256,6,64]{1,0,3,2:T(8,128)} %reshape.297, f32[16,256,6]{1,2,0:T(8,128)S(1)} %get-tuple-element.423, f32[16,256,6]{1,2,0:T(8,128)S(1)} %bitcast.280), kind=kOutput, calls=%fused_computation.118 | convolution fusion | flops 2419589120 | bytes 13828096 | tf_op jit(solution)/shard_map/transpose(jvp(csn,cshp->chpn))/dot_general | solution.py:51
  560.6 14.9 %multiply_reduce_fusion.7 = (f32[16,256,6]{1,2,0:T(8,128)S(1)}, f32[16,256,6]{1,2,0:T(8,128)S(1)}, f32[16,6,8,8,256]{4,3,2,1,0:T(8,128)}) fusion(f32[16,256,6,64]{1,0,3,2:T(8,128)} %reshape.297, f32[16,256,6]{1,2,0:T(8,128)S(1)} %bitcast.281, f32[16,6,64,256]{3,2,1,0:T(8,128)} %fusion.4, f32[16,256,6]{1,2,0:T(8,128)S(1)} %get-tuple-element.423, ...), kind=kOutput, calls=%fused_computation.71 | convolution fusion | flops 2426880000 | bytes 23461888 | tf_op jit(solution)/shard_map/transpose(jvp(csn,cshp->chpn))/dot_general | solution.py:51
  577.6 6.7 copy.297
  584.3 6.6 copy.298
  590.9 14.9 %reduce-window.16 = f32[16,6,2,128]{3,0,1,2:T(8,128)S(1)} reduce-window(f32[16,6,2,128]{3,0,1,2:T(8,128)S(1)} %copy.275, f32[]{:T(128)} %constant.113.clone.1), window={size=1x1x1x128 pad=0_0x0_0x0_0x0_127}, to_apply=%region_19.20 | reduce-window | flops 3121152 | bytes 196612 | tf_op jit(solution)/shard_map/reduce-window.2
  610.6 7.8 add_convert_fusion
  618.3 9.8 copy.268
  628.1 8.6 reshape.318
  636.7 4.7 all-to-all-start.4
  641.5 7.4 fusion.94
  648.9 7.9 fusion.67
  659.7 18.7 %all-to-all-done.4 = bf16[4,2,196608]{2,1,0:T(2,128)(2,1)} async-done(((bf16[4,2,196608]{2,1,0:T(2,128)(2,1)}), bf16[4,2,196608]{2,1,0:T(2,128)(2,1)}, u32[]{:S(2)}, u32[]{:S(2)}) %all-to-all-start.4) | async-done | bytes 3145760 | tf_op jit(solution)/shard_map/all_to_all | solution.py:173
  678.4 8.5 reshape.319
  686.9 9.5 copy.287
  700.9 4.6 copy.271
  705.5 20.3 %multiply_reduce_fusion.4 = (f32[1792]{0:T(1024)S(1)}, f32[1792]{0:T(1024)S(1)}, f32[1792]{0:T(1024)S(1)}, f32[1792]{0:T(1024)S(1)}, f32[1792]{0:T(1024)S(1)}, /*index=5*/f32[1024,1792]{1,0:T(8,128)}) fusion(f32[1027,1792]{1,0:T(8,128)} %copy-done.1, f32[1024,1792]{1,0:T(8,128)} %get-tuple-element.409, bf16[1024,1536]{1,0:T(8,128)(2,1)} %copy.271, ...), kind=kLoop, calls=%fused_computation.52 | loop fusion | flops 38526208 | bytes 47746048 | tf_op jit(solution)/shard_map/transpose(jvp())/reduce_sum | solution.py:81
  725.8 8.2 broadcast_multiply_fusion
  736.2 8.3 pad_add_fusion
  750.7 5.7 fusion.55
  756.5 7.0 fusion.107
  763.5 7.1 fusion.65
  776.3 8.9 fusion.39
  785.3 43.5 %all-reduce.13 = (f32[768]{0:T(1024)}, f32[4,1792]{1,0:T(4,128)}, f32[1792]{0:T(1024)}, f32[24]{0:T(128)}, f32[24]{0:T(128)}, /*index=5*/f32[24]{0:T(128)}, f32[1536]{0:T(1024)}) all-reduce(f32[768]{0:T(1024)S(1)} %get-tuple-element.350, f32[4,1792]{1,0:T(4,128)S(1)} %pad_add_fusion.2, ...), channel_id=1, replica_groups=mesh['dp'=8,'seq'=4] {'dp','seq'}, use_global_device_ids=true, to_apply=%region_24.25 | all-reduce | flops 11336 | bytes 90688 | tf_op jit(solution)/shard_map/psum | solution.py:219
  828.8 5.0 fusion.64
  833.8 186.2 %all-reduce.17.cloned.1.call-done = (f32[768,1536]{1,0:T(8,128)}, f32[768,1792]{1,0:T(8,128)}, f32[768,24]{0,1:T(8,128)}, f32[1536,768]{1,0:T(8,128)}) async-done(((f32[768,1536]{1,0:T(8,128)}, f32[768,1792]{1,0:T(8,128)}, f32[768,24]{0,1:T(8,128)}, f32[1536,768]{1,0:T(8,128)}), (f32[768,1536]{1,0:T(8,128)}, f32[768,1792]{1,0:T(8,128)}, f32[768,24]{0,1:T(8,128)}, ...) | async-done | bytes 15015952 | tf_op jit(solution)/shard_map/psum | solution.py:219
  1020.0 5.2 copy.394
  (414 shorter events, 212.8 us)
Async XLA Ops:
  7.2 108.7 %all-gather.2.cloned.1.call-start = ((), (), s32[]{:S(2)}) async-start(), calls=%async_computation.7 | async-start | bytes 2621440 | tf_op jit(solution)/shard_map/all_gather | solution.py:136
  9.8 7.5 copy-start.46
  14.9 3.2 collective-permute-start
  18.9 6.7 copy-start.1
  18.9 9.3 copy-start.27
  18.9 9.3 copy-start.44
  18.9 9.3 copy-start.61
  31.6 14.6 %all-to-all-start = ((bf16[1024,4,6]{0,2,1:T(8,128)(2,1)}), bf16[1024,4,6]{0,2,1:T(8,128)(2,1)S(1)}, u32[]{:S(2)}, u32[]{:S(2)}) async-start(bf16[1024,4,6]{0,2,1:T(8,128)(2,1)} %all_to_all.22), calls=%async_computation | async-start | bytes 131072 | tf_op jit(solution)/shard_map/all_to_all | solution.py:134
  46.2 5.4 copy-start.62
  46.2 6.0 copy-start.57
  46.2 42.5 %all-to-all-start.1 = ((bf16[1024,24,64]{0,2,1:T(8,128)(2,1)}), bf16[1024,24,64]{0,2,1:T(8,128)(2,1)}, u32[]{:S(2)}, u32[]{:S(2)}) async-start(bf16[1024,24,64]{0,2,1:T(8,128)(2,1)} %bitcast.271), calls=%async_computation.1 | async-start | bytes 6291456 | tf_op jit(solution)/shard_map/all_to_all | solution.py:133
  52.3 4.3 copy-start.53
  57.1 37.2 %copy-start.19 = (f32[16,6,256]{2,0,1:T(8,128)}, f32[16,6,256]{2,0,1:T(8,128)S(1)}, u32[]{:S(2)}) copy-start(f32[16,6,256]{2,0,1:T(8,128)S(1)} %copy_bitcast_fusion) | copy-start | bytes 294916
  57.3 36.9 %copy-start.25 = (f32[16,6,1]{1,0,2:T(8,128)}, f32[16,6,1]{1,0,2:T(8,128)S(1)}, u32[]{:S(2)}) copy-start(f32[16,6,1]{1,0,2:T(8,128)S(1)} %copy.292) | copy-start | bytes 1156
  118.6 11.3 %copy-start.6 = (bf16[4096,128]{1,0:T(8,128)(2,1)}, bf16[4096,128]{1,0:T(8,128)(2,1)S(1)}, u32[]{:S(2)}) copy-start(bf16[4096,128]{1,0:T(8,128)(2,1)S(1)} %get-tuple-element.421) | copy-start | bytes 3145732
  131.9 30.2 %copy-start.28 = (f32[16,6,256]{2,1,0:T(8,128)S(1)}, f32[16,6,256]{2,1,0:T(8,128)}, u32[]{:S(2)}) copy-start(f32[16,6,256]{2,1,0:T(8,128)} %get-tuple-element.425) | copy-start | bytes 294916
  131.9 30.2 %copy-start.40 = (pred[256,256]{1,0:T(8,128)(4,1)S(1)}, pred[256,256]{1,0:T(8,128)(4,1)}, u32[]{:S(2)}) copy-start(pred[256,256]{1,0:T(8,128)(4,1)} %iota_compare_fusion) | copy-start | bytes 196612
  159.7 33.9 %copy-start.51 = (f32[16,6]{1,0:T(8,128)}, f32[16,6]{1,0:T(8,128)S(1)}, u32[]{:S(2)}) copy-start(f32[16,6]{1,0:T(8,128)S(1)} %get-tuple-element.679) | copy-start | bytes 1156
  159.7 38.2 %slice-start = ((s8[6291456]{0:T(1024)(128)(4,1)}), s8[4194304]{0:T(1024)(128)(4,1)S(1)}, s32[]{:S(2)}) async-start(s8[6291456]{0:T(1024)(128)(4,1)} %bitcast.261), calls=%async_computation.10 | async-start | bytes 8388608
  162.2 31.5 %copy-start.3 = (bf16[4096,128]{1,0:T(8,128)(2,1)S(1)}, bf16[4096,128]{1,0:T(8,128)(2,1)}, u32[]{:S(2)}) copy-start(bf16[4096,128]{1,0:T(8,128)(2,1)} %get-tuple-element.422) | copy-start | bytes 3145732
  162.2 31.5 %copy-start.13 = (f32[16,6,64,128]{3,2,1,0:T(8,128)S(1)}, f32[16,6,64,128]{3,2,1,0:T(8,128)}, u32[]{:S(2)}) copy-start(f32[16,6,64,128]{3,2,1,0:T(8,128)} %get-tuple-element.215) | copy-start | bytes 9437188
  162.2 35.8 %slice-start.1 = ((s8[6291456]{0:T(1024)(128)(4,1)}), s8[2097152]{0:T(1024)(128)(4,1)S(1)}, s32[]{:S(2)}) async-start(s8[6291456]{0:T(1024)(128)(4,1)} %bitcast.261), calls=%async_computation.11 | async-start | bytes 4194304
  219.4 41.7 %all-to-all-start.2 = ((bf16[4,2,196608]{2,1,0:T(2,128)(2,1)}), bf16[4,2,196608]{2,1,0:T(2,128)(2,1)}, u32[]{:S(2)}, u32[]{:S(2)}) async-start(bf16[4,2,196608]{2,1,0:T(2,128)(2,1)} %reshape.316), calls=%async_computation.2 | async-start | bytes 6291456 | tf_op jit(solution)/shard_map/all_to_all | solution.py:142
  302.4 10.1 copy-start.21
  302.4 10.1 copy-start.48
  302.4 10.1 copy-start.55
  302.4 10.1 copy-start.59
  312.5 6.3 copy-start.15
  312.5 7.2 copy-start.9
  334.0 69.3 %all-to-all-start.3 = ((bf16[1024,24,64]{0,2,1:T(8,128)(2,1)}), bf16[1024,24,64]{0,2,1:T(8,128)(2,1)}, u32[]{:S(2)}, u32[]{:S(2)}) async-start(bf16[1024,24,64]{0,2,1:T(8,128)(2,1)} %bitcast.270), calls=%async_computation.3 | async-start | bytes 6291456 | tf_op jit(solution)/shard_map/all_to_all | solution.py:157
  338.7 366.8 %reduce-scatter.2.cloned.1.call-start = ((), (), s32[]{:S(2)}) async-start(), calls=%async_computation.8 | async-start | bytes 2621440 | tf_op jit(solution)/shard_map/reduce_scatter | solution.py:178
  409.3 13.7 %copy-start.41 = (pred[256,256]{1,0:T(8,128)(4,1)S(1)}, pred[256,256]{1,0:T(8,128)(4,1)}, u32[]{:S(2)}) copy-start(pred[256,256]{1,0:T(8,128)(4,1)} %iota_compare_fusion) | copy-start | bytes 196612
  415.3 7.7 copy-start.5
  415.3 7.7 copy-start.17
  415.3 7.7 copy-start.29
  468.7 5.5 copy-start.8
  474.2 12.3 %copy-start.4 = (bf16[4096,128]{1,0:T(8,128)(2,1)S(1)}, bf16[4096,128]{1,0:T(8,128)(2,1)}, u32[]{:S(2)}) copy-start(bf16[4096,128]{1,0:T(8,128)(2,1)} %get-tuple-element.422) | copy-start | bytes 3145732
  491.4 4.9 copy-start.7
  542.9 16.1 %copy-start.14 = (f32[16,256,128]{2,1,0:T(8,128)S(1)}, f32[16,256,128]{2,1,0:T(8,128)}, u32[]{:S(2)}) copy-start(f32[16,256,128]{2,1,0:T(8,128)} %bitcast_add_fusion.6) | copy-start | bytes 6291460
  560.6 14.9 %copy-start.20 = (f32[16,6,256]{2,0,1:T(8,128)S(1)}, f32[16,6,256]{2,0,1:T(8,128)}, u32[]{:S(2)}) copy-start(f32[16,6,256]{2,0,1:T(8,128)} %copy-done.19) | copy-start | bytes 294916
  560.6 14.9 %copy-start.26 = (f32[16,6,1]{1,0,2:T(8,128)S(1)}, f32[16,6,1]{1,0,2:T(8,128)}, u32[]{:S(2)}) copy-start(f32[16,6,1]{1,0,2:T(8,128)} %copy-done.25) | copy-start | bytes 1156
  584.3 22.0 %copy-start.54 = (f32[6]{0:T(128)S(1)}, f32[6]{0:T(128)}, u32[]{:S(2)}) copy-start(f32[6]{0:T(128)} %copy-done.53) | copy-start | bytes 76
  607.1 29.6 %all-to-all-start.5 = ((bf16[4,1024,6]{1,2,0:T(8,128)(2,1)}), bf16[4,1024,6]{1,2,0:T(8,128)(2,1)S(1)}, u32[]{:S(2)}, u32[]{:S(2)}) async-start(bf16[4,1024,6]{1,2,0:T(8,128)(2,1)} %copy.281), calls=%async_computation.6 | async-start | bytes 131072 | tf_op jit(solution)/shard_map/all_to_all | solution.py:174
  636.7 41.7 %all-to-all-start.4 = ((bf16[4,2,196608]{2,1,0:T(2,128)(2,1)}), bf16[4,2,196608]{2,1,0:T(2,128)(2,1)}, u32[]{:S(2)}, u32[]{:S(2)}) async-start(bf16[4,2,196608]{2,1,0:T(2,128)(2,1)} %reshape.318), calls=%async_computation.5 | async-start | bytes 6291456 | tf_op jit(solution)/shard_map/all_to_all | solution.py:173
  641.4 378.6 %all-reduce.17.cloned.1.call-start = ((), (), s32[]{:S(2)}) async-start(), calls=%async_computation.9 | async-start | bytes 30031872 | tf_op jit(solution)/shard_map/psum | solution.py:219
  641.5 7.5 copy-start.22
  641.5 7.4 copy-start.49
  641.5 7.4 copy-start.56
  648.9 8.0 copy-start.30
  705.5 20.3 %copy-start.33 = (f32[1792]{0:T(1024)S(1)}, f32[1792]{0:T(1024)}, u32[]{:S(2)}) copy-start(f32[1792]{0:T(1024)} %copy-done.32) | copy-start | bytes 21508
  705.5 20.3 %copy-start.35 = (f32[1792]{0:T(1024)S(1)}, f32[1792]{0:T(1024)}, u32[]{:S(2)}) copy-start(f32[1792]{0:T(1024)} %copy-done.34) | copy-start | bytes 21508
  705.5 20.3 %copy-start.37 = (f32[1792]{0:T(1024)S(1)}, f32[1792]{0:T(1024)}, u32[]{:S(2)}) copy-start(f32[1792]{0:T(1024)} %copy-done.36) | copy-start | bytes 21508
  705.5 20.3 %copy-start.39 = (f32[1792]{0:T(1024)S(1)}, f32[1792]{0:T(1024)}, u32[]{:S(2)}) copy-start(f32[1792]{0:T(1024)} %copy-done.38) | copy-start | bytes 21508
  734.9 12.7 %collective-permute-start.1 = (f32[3,1792]{1,0:T(4,128)S(1)}, f32[3,1792]{1,0:T(4,128)S(1)}, u32[]{:S(2)}, u32[]{:S(2)}) collective-permute-start(f32[3,1792]{1,0:T(4,128)S(1)} %pad_add_fusion.1), channel_id=1, source_target_pairs={{1,0},{2,1},{3,2},{5,4},{6,5},{7,6},{9,8},{10,9},{11,10},{13,12},{... | collective-permute-start | bytes 64520 | tf_op jit(solution)/shard_map/ppermute | solution.py:21
  744.6 4.5 copy-start.2
  756.4 7.1 copy-start.12
  756.4 7.1 copy-start.60
  770.6 4.4 copy-start.24
  770.6 4.6 copy-start.58
  770.6 4.9 copy-start.45
  776.3 9.0 copy-start.50
  776.3 52.5 %copy-start.43 = (f32[1024]{0:T(1024)S(1)}, f32[1024]{0:T(1024)}, u32[]{:S(2)}) copy-start(f32[1024]{0:T(1024)} %copy-done.42) | copy-start | bytes 12292
  1020.0 5.2 copy-start.16
  1020.0 9.3 slice-start.2
  (14 other events, 30.4 us)
Sparse Core Ops, SparseCore 0:
  28.4 27.1 all-gather.1
  560.7 33.0 reduce-scatter.1
  756.6 263.4 all-reduce.16
where the time goes:
time: 1050 us; the launch traced here: 1040 us
  waiting for transfers between devices  272 us (26%)
  local copies, waits for them, and re-layouts  241 us (23%)
  matrix products  234 us (22%)
  other arithmetic  198 us (19%)
  blocking collectives  43.5 us (4%)
  starting transfers between devices  32.8 us (3%)
  between operations  15.7 us (1%)
    psum x1, waiting for transfers between devices, local(): lax.psum((grad_norm_gain, grad_w_z, grad_w_xbc, grad_w_dt, grad_conv_weig...  186 us
    dot_general x3, matrix products, state_scan(): within = jnp.einsum('chts,cshp->cthp', scores, inflow, precision=HIGH)  77.1 us
    unnamed x142, local copies, waits for them, and re-layouts  50.9 us
    psum x1, blocking collectives, local(): lax.psum((grad_norm_gain, grad_w_z, grad_w_xbc, grad_w_dt, grad_conv_weig...  43.5 us
    dot_general x3, matrix products, state_scan(): jnp.einsum('csn,cshp->chpn', b_groups, weighted, precision=HIGH)  42.2 us
    all_to_all x1, waiting for transfers between devices, local(): lax.all_to_all(y_heads, 'seq', split_axis=0, concat_axis=1, tiled=True)  35.7 us
    dynamic_update_slice x48, other arithmetic, state_scan(): lax.scan(advance, zero_state, (jnp.exp(final_log), group_state))  33.5 us
    add x32, other arithmetic, advance(): return (factor[:, None, None] * state_in + added, state_in)  32.4 us
  transfers between devices with their start and end apart: 11, of which 5 were waited for; matrix products, arithmetic and copies ran while one was open for 26% of the time, Pallas kernels for 0%

commit v1 on v0

v1 whole, which is shorter than its diff:
```python
import jax
import jax.numpy as jnp
from jax import lax
from jax.experimental import pallas as pl
from jax.experimental.pallas import tpu as pltpu
from jax.sharding import PartitionSpec as P

HEAD_DIM = 64
STATE = 128
CONV = 4
EPSILON = 1e-05
LOG2E = 1.4426950408889634
BLOCK = 256
SUB = 128
SUBS = BLOCK // SUB
LANES = 128
WIDE = 256
PIECE = 512
RIM = 16
F32 = jnp.float32
BF16 = jnp.bfloat16
VMEM_LIMIT = 65200 * 1024
MESH = pl.DeviceIdType.MESH
RATE, DT_BIAS, SKIP, REAL = range(4)


def dot(left, right):
    return jnp.dot(left, right, preferred_element_type=F32)


def dot_t(left, right):
    return lax.dot_general(left, right, (((1,), (1,)), ((), ())), preferred_element_type=F32)


def t_dot(left, right):
    return lax.dot_general(left, right, (((0,), (0,)), ((), ())), preferred_element_type=F32)


def split_dot(left, right):
    high = left.astype(BF16)
    low = (left - high.astype(F32)).astype(BF16)
    return dot(high, right) + dot(low, right)


def split_dot_t(left, right):
    high = left.astype(BF16)
    low = (left - high.astype(F32)).astype(BF16)
    return dot_t(high, right) + dot_t(low, right)


def flip(value):
    return value.astype(F32).T.astype(BF16)


def sigmoid(value):
    return 0.5 * jnp.tanh(0.5 * value) + 0.5


def fold(value):
    return jnp.sum(value.reshape(-1, 8, value.shape[1]), axis=0)


def grid2(size):
    return (
        lax.broadcasted_iota(jnp.int32, (size, size), 0),
        lax.broadcasted_iota(jnp.int32, (size, size), 1),
    )


def lower_ones(size):
    row, col = grid2(size)
    return jnp.where(row >= col, 1.0, 0.0).astype(BF16)


def half_mask():
    return lax.broadcasted_iota(jnp.int32, (SUB, LANES), 1) < HEAD_DIM


def pair_diag(value, first_half):
    zero = jnp.zeros_like(value)
    return jnp.concatenate(
        [jnp.where(first_half, value, zero), jnp.where(first_half, zero, value)], axis=0
    )


def set_spread(spread):
    row = lax.broadcasted_iota(jnp.int32, spread.shape, 0)
    head = lax.broadcasted_iota(jnp.int32, spread.shape, 1) // HEAD_DIM
    spread[...] = jnp.where((row % 32 == head) & (row < 96), 1.0, 0.0).astype(BF16)


def parts(value):
    value = jnp.where(lax.broadcasted_iota(jnp.int32, value.shape, 1) < 32, value, 0.0)
    high = value.astype(BF16).astype(F32)
    rest = value - high
    mid = rest.astype(BF16).astype(F32)
    low = (rest - mid).astype(BF16).astype(F32)
    return (high + pltpu.roll(mid, 32, 1) + pltpu.roll(low, 64, 1)).astype(BF16)


def tile(index, width=LANES):
    return pl.ds(pl.multiple_of(index * width, width), width)


def chunks(width):
    return [slice(start, start + WIDE) for start in range(0, width, WIDE)]


def norm_rows(rows):
    value = rows.astype(F32)
    return value, lax.rsqrt(jnp.mean(value * value, axis=-1, keepdims=True) + EPSILON)


def normed_of(rows, gain):
    value, rms = norm_rows(rows)
    return (value * rms * gain).astype(BF16)


def head_row(value):
    row = value.reshape(1, -1)
    return jnp.concatenate([row, jnp.zeros((1, LANES - row.shape[1]), F32)], axis=1)


def set_rate(heads, a_log_ref):
    heads[RATE : RATE + 1, :] = head_row(-jnp.exp(a_log_ref[...]) * LOG2E)


def set_conv(conv, weight_ref, bias_ref):
    conv[0:CONV, :] = weight_ref[...]
    conv[CONV : CONV + 1, :] = bias_ref[...].reshape(1, -1)


def set_step_weight(weight, wdt_ref):
    weight[...] = jnp.zeros_like(weight)
    weight[0 : wdt_ref.shape[0], :] = wdt_ref[...]


def places():
    dp, seq = lax.axis_index("dp"), lax.axis_index("seq")
    core_size = 2
    y_size = lax.axis_size("seq") // core_size
    x_size = y_size if lax.axis_size("dp") % y_size == 0 else 1
    z_size = lax.axis_size("dp") // x_size
    x, z = lax.rem(dp, x_size), lax.div(dp, x_size)
    core, y = lax.rem(seq, core_size), lax.div(seq, core_size)
    return {
        "core": (core_size, core, lambda p: {"dp": dp, "seq": y * core_size + p}),
        "y": (y_size, y, lambda p: {"dp": dp, "seq": p * core_size + core}),
        "x": (x_size, x, lambda p: {"dp": z * x_size + p, "seq": seq}),
        "z": (z_size, z, lambda p: {"dp": p * x_size + x, "seq": seq}),
        "seq": (lax.axis_size("seq"), seq, lambda p: {"dp": dp, "seq": p}),
    }


def axis_sizes():
    y_size = lax.axis_size("seq") // 2
    return [2, y_size, y_size, lax.axis_size("dp") // y_size]


def greet(axes, names):
    barrier = pltpu.get_barrier_semaphore()
    count = 0
    for name in names:
        size, index, at = axes[name]
        for k in range(1, size):
            pl.semaphore_signal(barrier, inc=1, device_id=at(lax.rem(index + k, size)), device_id_type=MESH)
            count += 1
    pl.semaphore_wait(barrier, count)


def state_copies(axes, value, slots, send_sems, recv_sems):
    size, index, at = axes["seq"]
    return [
        pltpu.make_async_remote_copy(
            src_ref=value,
            dst_ref=slots.at[index],
            send_sem=send_sems.at[k - 1],
            recv_sem=recv_sems.at[k - 1],
            device_id=at(lax.rem(index + k, size)),
            device_id_type=MESH,
        )
        for k in range(1, size)
    ]


def two_level(axes, value, pair, chip, chips, send_sems, recv_sems):
    _, core, at_core = axes["core"]
    size, y, at_y = axes["y"]
    width = value.shape[-1] // 2
    half = pl.ds(pl.multiple_of(core * width, LANES), width)

    def remote(source, target, device, n):
        return pltpu.make_async_remote_copy(
            src_ref=source, dst_ref=target, send_sem=send_sems.at[n], recv_sem=recv_sems.at[n],
            device_id=device, device_id_type=MESH,
        )

    first = [remote(value, pair, at_core(1 - core), 0)]
    second = [remote(chip, chips.at[y, :, half], at_y(lax.rem(y + k, size)), k) for k in range(1, size)]
    received = [chips.at[lax.rem(y + size - k, size), :, half] for k in range(1, size)]
    third = [remote(ref, ref, at_core(1 - core), size + n) for n, ref in enumerate(received)]
    return half, first, second, third


def shift_copy(axes, source, target, by, send_sem, recv_sem):
    size, index, at = axes["seq"]
    return pltpu.make_async_remote_copy(
        src_ref=source, dst_ref=target, send_sem=send_sem, recv_sem=recv_sem,
        device_id=at(lax.rem(index + by + size, size)), device_id_type=MESH,
    )


def padded(count, unit):
    return -(-count // unit) * unit


def piece_of(rows):
    return max(n for n in range(16, 513, 16) if rows % n == 0)


class Job:
    def __init__(self, src, dst, recv, recv_base, base, rows, order, axes, send_sems, recv_sems, own_sem):
        self.src, self.dst, self.recv = src, dst, recv
        self.send_sems, self.recv_sems = send_sems, recv_sems
        self.axes = [axes[name] for name in order]
        self.spans = [(base, rows)]
        self.slots = []
        for size, index, _ in self.axes:
            at, span = self.spans[-1]
            part = span // size
            self.spans.append((pl.multiple_of(at + index * part, 16), part))
            self.slots.append(recv_base)
            recv_base += (size - 1) * part
        self.stages = 2 * len(self.axes)
        self.end = base + rows
        own, part = self.spans[-1]
        self.result = recv.at[pl.ds(self.slots[-1], part)]
        self.keep = pltpu.make_async_copy(self.result, dst.at[pl.ds(own, part)], own_sem)

    def copies(self, stage):
        down = stage < len(self.axes)
        level = stage if down else self.stages - 1 - stage
        size, index, at = self.axes[level]
        base, _ = self.spans[level]
        own, part = self.spans[level + 1]
        result = []
        for k in range(1, size):
            partner = lax.rem(index + k, size)
            if down:
                if level == 0:
                    source = self.src.at[pl.ds(pl.multiple_of(base + partner * part, 16), part)]
                else:
                    held = self.slots[level - 1]
                    source = self.recv.at[pl.ds(pl.multiple_of(held + partner * part, 16), part)]
                target = self.recv.at[pl.ds(self.slots[level] + (k - 1) * part, part)]
            else:
                target = self.dst.at[pl.ds(own, part)]
                source = self.result if stage == len(self.axes) else target
            result.append(
                pltpu.make_async_remote_copy(
                    src_ref=source,
                    dst_ref=target,
                    send_sem=self.send_sems.at[stage, k - 1],
                    recv_sem=self.recv_sems.at[stage, k - 1],
                    device_id=at(partner),
                    device_id_type=MESH,
                )
            )
        return result

    def start(self, stage):
        for copy in self.copies(stage):
            copy.start()

    def move(self, stage):
        if stage > 0:
            self.finish(stage - 1)
        if stage < self.stages:
            self.start(stage)

    def finish(self, stage):
        for copy in self.copies(stage):
            copy.wait()
        if stage == len(self.axes):
            self.keep.wait()
        if stage >= len(self.axes):
            return
        size, index, _ = self.axes[stage]
        own, part = self.spans[stage + 1]
        slot = self.slots[stage]
        step = piece_of(part)

        @pl.loop(0, part // step)
        def _(i):
            def rows(start):
                return pl.ds(pl.multiple_of(start + i * step, 16), step)

            if stage == 0:
                total = self.src[rows(own), :].astype(F32)
            else:
                total = self.recv[rows(self.slots[stage - 1] + index * part), :].astype(F32)
            for k in range(size - 1):
                total = total + self.recv[rows(slot + k * part), :].astype(F32)
            self.recv[rows(slot), :] = total.astype(BF16)

        if stage == len(self.axes) - 1:
            self.keep.start()


class VectorJob:
    def __init__(self, total, recv, order, axes, send_sems, recv_sems):
        self.total, self.recv, self.send_sems, self.recv_sems = total, recv, send_sems, recv_sems
        self.axes = [axes[name] for name in order]
        self.slots = [sum(axis[0] for axis in self.axes[:i]) for i in range(len(self.axes))]

    def copies(self, stage):
        size, index, at = self.axes[stage]
        slot = self.slots[stage] + index
        return [
            pltpu.make_async_remote_copy(
                src_ref=self.recv.at[slot],
                dst_ref=self.recv.at[slot],
                send_sem=self.send_sems.at[stage, k - 1],
                recv_sem=self.recv_sems.at[stage, k - 1],
                device_id=at(lax.rem(index + k, size)),
                device_id_type=MESH,
            )
            for k in range(1, size)
        ]

    def start(self, stage):
        self.recv[self.slots[stage] + self.axes[stage][1]] = self.total[...]
        for copy in self.copies(stage):
            copy.start()

    def finish(self, stage):
        for copy in self.copies(stage):
            copy.wait()
        slot = self.slots[stage]
        total = self.recv[slot]
        for k in range(1, self.axes[stage][0]):
            total = total + self.recv[slot + k]
        self.total[...] = total


EARLY_JOBS = (9, 9, 9, 9)
LATE_JOBS = (3, 3, 3, 3, 3, 3, 2, 2)
MOST_JOBS = 8
ORDERS = (("core", "x", "y", "z"), ("core", "y", "x", "z"))
STAGES = 8


def jobs_of(sizes, src, dst, recv, axes, send_sems, recv_sems, own_sems):
    unit = 16 * lax.axis_size("dp") * lax.axis_size("seq")
    units = src.shape[0] // unit
    if sum(sizes) != units:
        sizes = [1] * units
    jobs = []
    base = 0
    for n, size in enumerate(sizes):
        rows = size * unit
        jobs.append(
            Job(
                src, dst, recv, base, base, rows, ORDERS[n % 2], axes, send_sems.at[n], recv_sems.at[n], own_sems.at[n]
            )
        )
        base += rows
    return jobs


def job_sems():
    return pltpu.SemaphoreType.DMA((JOBS, STAGES, max(axis_sizes()) - 1))


def pack_slabs(packed_ref, at, rows, first, value):
    count, width = value.shape
    for n in range(width // LANES):
        start = at + n * rows + first
        packed_ref[start : start + count, :] = value[:, n * LANES : (n + 1) * LANES].astype(BF16)


def enter_kernel(
    tok_ref, tail_ref, last_ref, gain_ref, wx_ref, wdt_in, weight_ref, bias_ref, dtb_ref, a_log_ref,
    normed_ref, xbc_ref, x_ref, bc_ref, dt_ref, sig_ref, added_ref, state_ref, logd_ref, xhalo_ref,
    product, spread, ext, state, suffix, prev, halo, xbc_send, xbc_halo, heads_ref, conv_ref, wdt_ref,
    halo_send, halo_recv, xbc_sems,
):
    step = pl.program_id(0)
    steps = pl.num_programs(0)
    inner = x_ref.shape[1]
    width = xbc_ref.shape[1]
    features = tok_ref.shape[2]
    axes = places()
    shift = shift_copy(axes, last_ref.at[0], halo, 1, halo_send, halo_recv)
    xbc_shift = shift_copy(axes, xbc_send, xbc_halo, 1, xbc_sems.at[0], xbc_sems.at[1])

    @pl.when(step == 0)
    def _():
        greet(axes, ("seq",))
        shift.start()
        set_spread(spread)
        set_rate(heads_ref, a_log_ref)
        heads_ref[DT_BIAS : DT_BIAS + 1, :] = head_row(dtb_ref[...])
        heads_ref[REAL : REAL + 1, :] = head_row(jnp.ones_like(dtb_ref))
        set_conv(conv_ref, weight_ref, bias_ref)
        set_step_weight(wdt_ref, wdt_in)
        state[...] = jnp.zeros_like(state)
        suffix[...] = jnp.zeros_like(suffix)

    @pl.when(step < steps - 1)
    def _():
        prev[...] = tail_ref[0]

    @pl.when(step == steps - 1)
    def _():
        shift.wait()
        prev[...] = jnp.where(axes["seq"][1] == 0, jnp.zeros_like(prev), halo[...])

    gain = gain_ref[...].reshape(1, -1)
    normed = normed_of(tok_ref[0], gain)
    both = jnp.concatenate([normed_of(prev[...], gain), normed], axis=0)
    normed_ref[...] = normed
    product[...] = dot(both, wx_ref[...])
    for n in range(width // LANES):
        lanes = slice(n * LANES, (n + 1) * LANES)
        part = product[:, lanes].astype(BF16)
        xbc_ref[:, lanes] = part[RIM:]
        ext[n] = part.astype(F32)

    @pl.when(step == 0)
    def _():
        xbc_send[...] = xbc_ref[BLOCK - RIM :, :]
        xbc_shift.start()

    real = heads_ref[REAL : REAL + 1, :]
    dt_raw = dot_t(normed, wdt_ref[...]) + heads_ref[DT_BIAS : DT_BIAS + 1, :]
    softplus = jnp.maximum(dt_raw, 0.0) + jnp.log1p(jnp.exp(-jnp.abs(dt_raw)))
    dt_low = (softplus * real).astype(BF16)
    dt_ref[...] = dt_low
    sig_ref[...] = sigmoid(dt_raw)

    def conv(lane, dst_ref, dst_lane):
        lanes = tile(lane)
        taps = [conv_ref[k : k + 1, lanes] for k in range(CONV)]
        bias = conv_ref[CONV : CONV + 1, lanes]
        for row in range(0, BLOCK, 64):
            total = bias
            for k in range(CONV):
                at = row + RIM - (CONV - 1) + k
                total = total + taps[k] * ext[lane, at : at + 64, :]
            dst_ref[row : row + 64, tile(dst_lane)] = (total * sigmoid(total)).astype(BF16)

    for lane in range(2):
        conv(inner // LANES + lane, bc_ref, lane)

    @pl.loop(0, inner // LANES)
    def _(lane):
        conv(lane, x_ref, lane)

    ones = lower_ones(SUB)
    factors = []
    finals = []
    for sub in range(SUBS):
        dt_sub = dt_low[sub * SUB : (sub + 1) * SUB]
        run = dot(ones, dt_sub) * heads_ref[RATE : RATE + 1, :]
        final = run[SUB - 1 : SUB]
        factors.append(parts(jnp.exp2(final - run) * dt_sub.astype(F32)))
        finals.append(parts(jnp.broadcast_to(final, (8, LANES))))
    b_flip = [flip(bc_ref[sub * SUB : (sub + 1) * SUB, :STATE]) for sub in range(SUBS)]
    product[:, :inner] = dot(jnp.concatenate(factors + finals, axis=0), spread[...])
    for sub in reversed(range(SUBS)):
        rows = slice(sub * SUB, (sub + 1) * SUB)
        at = SUBS * SUB + 8 * sub
        weighted = (product[rows, :inner] * x_ref[rows, :].astype(F32)).astype(BF16)
        added = dot(b_flip[sub], weighted)
        added_ref[sub] = added.astype(BF16)
        state[...] += jnp.exp2(suffix[0:1, :]) * added
        suffix[...] += product[at : at + 8, :inner]

    @pl.when(step == steps - 1)
    def _():
        state_ref[...] = state[...].astype(BF16)
        logd_ref[...] = suffix[...]
        xbc_shift.wait()
        xhalo_ref[...] = jnp.where(axes["seq"][1] == 0, jnp.zeros_like(xbc_halo), xbc_halo[...])


def middle_kernel(
    len_ref, tok_ref, cot_ref, normed_ref, x_ref, bc_ref, dt_ref, added_ref, state_ref, logd_ref,
    wz_ref, wo_ref, gain_ref, a_log_ref, skip_in,
    out_ref, gy_ref, gz_ref, starts_ref, rowdot_ref, adj_ref, pack_ref, ggain_ref, logds_ref, norm_t_ref,
    wide, spread, scan, state, prefix, skip, gate, go, o_all, gz_all, gb_all, norm_t, adj, ggain, pair_state, chip_state, chips, logds,
    heads_ref, gains_ref, slot_send, slot_recv, log_send, log_recv,
):
    step = pl.program_id(0)
    steps = pl.num_programs(0) // 2
    inner = x_ref.shape[1]
    features = tok_ref.shape[2]
    tok_rows = steps * BLOCK
    axes = places()
    count, me, _ = axes["seq"]
    core = axes["core"][1]
    y_count, y, _ = axes["y"]
    half, pair_copies, chip_copies, half_copies = two_level(
        axes, state_ref, pair_state, chip_state, chips, slot_send, slot_recv
    )
    pair_copies += state_copies(axes, logd_ref, logds, log_send, log_recv)
    ones = lower_ones(SUB)

    @pl.when(step == 0)
    def _():
        greet(axes, ("seq",))
        for copy in pair_copies:
            copy.start()
        logds[me] = logd_ref[...]
        set_spread(spread)
        set_rate(heads_ref, a_log_ref)
        heads_ref[SKIP : SKIP + 1, :] = head_row(skip_in[...])
        gains_ref[1:2, :] = gain_ref[...].reshape(1, -1)
        prefix[...] = jnp.zeros_like(prefix)
        adj[...] = jnp.zeros_like(adj)
        ggain[...] = jnp.zeros_like(ggain)
        for lanes in chunks(inner):
            skip[:, lanes] = dot(
                parts(jnp.broadcast_to(heads_ref[SKIP : SKIP + 1, :], (8, LANES))), spread[:, lanes]
            )

    @pl.when(step < steps)
    def _():
        row_i, col_i = grid2(SUB)
        causal = row_i >= col_i
        first_half = half_mask()
        for sub in range(SUBS):
            rows = slice(sub * SUB, (sub + 1) * SUB)
            dt_low = dt_ref[rows]
            meet = jnp.where(causal, dot_t(bc_ref[rows, STATE:], bc_ref[rows, :STATE]), 0.0)
            run = dot(ones, dt_low) * heads_ref[RATE : RATE + 1, :]
            run_t = run.T
            first_row = step * BLOCK + sub * SUB
            all_rows = pl.ds(pl.multiple_of(first_row, SUB), SUB)
            live = me * tok_rows + first_row + lax.broadcasted_iota(jnp.int32, (SUB, 1), 0) < len_ref[0]
            g_branch = jnp.where(live, cot_ref[0, rows, :], jnp.zeros((SUB, features), BF16))
            gb_all[all_rows, :] = g_branch
            normed = normed_ref[rows, :]
            norm_t[:, all_rows] = flip(normed)
            wide[:SUB, :] = dot(dt_low, spread[...])
            if sub == SUBS - 1:
                block_rows = tile(step, BLOCK)
                gate[block_rows, :] = dot(normed_ref[...], wz_ref[...])
                go[block_rows, :] = dot_t(gb_all[block_rows, :], wo_ref[...])
            for pair in range(inner // LANES):
                lanes = slice(pair * LANES, (pair + 1) * LANES)
                inflow = wide[:SUB, lanes] * x_ref[rows, lanes].astype(F32)
                scores = []
                for head in (2 * pair, 2 * pair + 1):
                    gap = jnp.minimum(run[:, head : head + 1] - run_t[head : head + 1, :], 0.0)
                    scores.append((jnp.exp2(gap) * meet).astype(BF16))
                scan[step, rows, lanes] = dot(
                    jnp.concatenate(scores, axis=1), pair_diag(inflow.astype(BF16), first_half)
                )

    @pl.when(step == 0)
    def _():
        for copy in pair_copies:
            copy.wait()
        mine, other = state_ref[:, half].astype(F32), pair_state[:, half].astype(F32)
        decay = jnp.exp2(logds[2 * y + 1, 0:1, half])
        chip_state[...] = jnp.where(core == 0, decay * mine + other, decay * other + mine).astype(BF16)
        for copy in chip_copies:
            copy.start()

    @pl.when(step == steps // 2)
    def _():
        for copy in chip_copies:
            copy.wait()
        for copy in half_copies:
            copy.start()

    @pl.when(step == steps)
    def _():
        for copy in half_copies:
            copy.wait()
        logds_ref[...] = logds[...]
        for lanes in chunks(inner):
            total = jnp.zeros((STATE, WIDE), F32)
            for chip in range(y_count):
                decay = jnp.exp2(logds[2 * chip, 0:1, lanes] + logds[2 * chip + 1, 0:1, lanes])
                total = jnp.where(chip < y, decay * total + chips[chip, :, lanes].astype(F32), total)
            decay = jnp.exp2(logds[2 * y, 0:1, lanes])
            state[:, lanes] = jnp.where(core == 1, decay * total + pair_state[:, lanes].astype(F32), total)

    @pl.when(step >= steps)
    def _():
        block = step - steps
        live = (
            me * tok_rows + block * BLOCK + lax.broadcasted_iota(jnp.int32, (BLOCK, 1), 0) < len_ref[0]
        )
        adj_factors = []
        for sub in range(SUBS):
            rows = slice(sub * SUB, (sub + 1) * SUB)
            c_out = bc_ref[rows, STATE:]
            run = dot(ones, dt_ref[rows]) * heads_ref[RATE : RATE + 1, :]
            final = run[SUB - 1 : SUB]
            factors = [parts(jnp.exp2(run)), parts(jnp.broadcast_to(jnp.exp2(final), (16, LANES)))]
            adj_factors.append(parts(jnp.exp2(run + prefix[0:1, :])))
            prefix[...] += final
            low = state[...].astype(BF16)
            starts_ref[sub] = low
            wide[...] = dot(jnp.concatenate(factors, axis=0), spread[...])
            scan[block, rows, :] += wide[:SUB, :] * dot(c_out, low)
            state[...] = wide[SUB : SUB + 1, :] * state[...] + added_ref[sub].astype(F32)
        base = pl.multiple_of(block * BLOCK, BLOCK)

        @pl.loop(0, BLOCK // 32)
        def _(chunk):
            rows = tile(chunk, 32)
            all_rows = pl.ds(pl.multiple_of(base + chunk * 32, 32), 32)
            square = jnp.zeros((32, LANES), F32)
            cross = jnp.zeros((32, LANES), F32)
            for lane in range(inner // LANES):
                lanes = slice(lane * LANES, (lane + 1) * LANES)
                y = (scan[block, rows, lanes] + skip[0:1, lanes] * x_ref[rows, lanes].astype(F32)).astype(BF16)
                o_all[all_rows, lanes] = y
                pre = gate[all_rows, lanes]
                gated = y.astype(F32) * (pre * sigmoid(pre))
                square += gated * gated
                cross += go[all_rows, lanes] * gains_ref[1:2, lanes] * gated
            rms = lax.rsqrt(jnp.sum(square, axis=-1, keepdims=True) * (1.0 / inner) + EPSILON)
            pull = jnp.sum(cross, axis=-1, keepdims=True) * (1.0 / inner) * rms * rms * rms
            rms = jnp.broadcast_to(rms, (32, LANES))
            pull = jnp.broadcast_to(pull, (32, LANES))
            for lane in range(inner // LANES):
                lanes = slice(lane * LANES, (lane + 1) * LANES)
                y = o_all[all_rows, lanes].astype(F32)
                pre = gate[all_rows, lanes]
                sig = sigmoid(pre)
                silu = pre * sig
                gated = y * silu
                gain = gains_ref[1:2, lanes]
                g_o = go[all_rows, lanes]
                unit = gated * rms
                o_all[all_rows, lanes] = (unit * gain).astype(BF16)
                ggain[:, lanes] += fold(g_o * unit)
                g_gated = rms * (g_o * gain) - pull * gated
                g_y = (g_gated * silu).astype(BF16)
                gy_ref[rows, lanes] = g_y
                g_z = (g_gated * y * (sig + silu * (1.0 - sig))).astype(BF16)
                gz_ref[rows, lanes] = g_z
                gz_all[all_rows, lanes] = g_z
                go[all_rows, lanes] = g_y.astype(F32) * scan[block, rows, lanes]

        branch = dot(o_all[tile(block, BLOCK), :], wo_ref[...])
        out_ref[0] = (tok_ref[0].astype(F32) + jnp.where(live, branch, 0.0)).astype(BF16)
        product = go[tile(block, BLOCK), :]
        high = product.astype(BF16)
        low = (product - high.astype(F32)).astype(BF16)
        head_sums = dot_t(jnp.concatenate([high, low], axis=0), spread[...])
        rowdot_ref[...] = head_sums[:BLOCK] + head_sums[BLOCK:]
        c_flip = jnp.concatenate([flip(bc_ref[sub * SUB : (sub + 1) * SUB, STATE:]) for sub in range(SUBS)], axis=1)
        factor = jnp.concatenate(adj_factors, axis=0)
        scaled = (dot(factor, spread[...]) * gy_ref[...].astype(F32)).astype(BF16)
        adj[...] += dot(c_flip, scaled)

    @pl.when(step == 2 * steps - 1)
    def _():
        norm_t_ref[...] = norm_t[...]
        adj_ref[...] = adj[...].astype(BF16)
        ggain_ref[...] = ggain[...]
        for lanes in chunks(inner):
            o_flip = flip(o_all[:, lanes])
            pack_slabs(pack_ref, 0, inner, lanes.start, dot(o_flip, gb_all[...]))
        for start in range(0, features, BLOCK):
            part = dot(norm_t[start : start + BLOCK, :], gz_all[...])
            pack_slabs(pack_ref, inner * features // LANES, features, start, part)
        used = 2 * inner * features // LANES
        if pack_ref.shape[0] > used:
            pack_ref[used:, :] = jnp.zeros((pack_ref.shape[0] - used, LANES), BF16)


def vector_rows(features, width, inner):
    counts = (features // LANES, CONV * width // LANES, width // LANES, inner // LANES, 1, 1, 1)
    starts = [sum(counts[:n]) for n in range(len(counts))]
    return starts, padded(sum(counts), 8)


def back_kernel(
    x_row, x_col, gy_row, gy_col, bc_ref, dt_ref, sig_ref, rowdot_ref, starts_ref, xbc_ref, xhalo_ref, xbc_rest, xhalo_rest, adj_ref,
    logds_ref, early_ref, ggain_ref, tok_ref, cot_ref, norm_t_in, gz_in, wz_in, wx_in, wdt_in,
    gain_ref, weight_ref, bias_ref, a_log_ref, skip_in,
    grad_ref, early_out, late_out, vec_out,
    spread, gather, ginf, factors, finals, c_flip, g_bc, x_ginf, column, d_final, skip, act, ext, gconv, gx_all, gdt_all,
    last, rim_send, rim_recv, gcw, gcb, gdtb, grate, gskip, gng, pair_adj, chip_adj, chips, early_recv, late_src, late_recv, vec, vec_recv,
    heads_ref, conv_ref, wdt_ref, norm_t, gz_ref, wz_ref, wx_ref,
    early_sems, late_sems, own_sems, vec_sems, slot_send, slot_recv, rim_sems, load_sems,
):
    step = pl.program_id(0)
    tok_rows, features = gx_all.shape[0], tok_ref.shape[2]
    inner = wz_ref.shape[1]
    width = wx_ref.shape[1]
    blocks = tok_rows // BLOCK
    subs = tok_rows // SUB
    pieces = inner // PIECE
    slab_rows = PIECE // LANES * features
    gn = ginf.at[:, pl.ds(0, features)]
    channel_step = blocks
    product_step = blocks + pieces
    norm_step = product_step + 1
    axes = places()
    count, me, _ = axes["seq"]
    core = axes["core"][1]
    y_count, y, _ = axes["y"]
    half, pair_copies, chip_copies, half_copies = two_level(
        axes, adj_ref, pair_adj, chip_adj, chips, slot_send, slot_recv
    )
    early = jobs_of(
        EARLY_JOBS, early_ref, early_out, early_recv, axes, early_sems.at[0], early_sems.at[1], own_sems.at[0]
    )
    late = jobs_of(LATE_JOBS, late_src, late_out, late_recv, axes, late_sems.at[0], late_sems.at[1], own_sems.at[1])
    vector = VectorJob(vec, vec_recv, ORDERS[0], axes, vec_sems.at[0], vec_sems.at[1])
    ones = lower_ones(SUB)
    row_i, col_i = grid2(SUB)
    later = row_i <= col_i

    loads = [
        pltpu.make_async_copy(source, target, load_sems.at[n])
        for n, (source, target) in enumerate(
            ((norm_t_in, norm_t), (gz_in, gz_ref), (wz_in, wz_ref), (wx_in, wx_ref))
        )
    ]

    channel_time = blocks * WITHIN_TIME
    product_time = channel_time + pieces * CHANNEL_TIME
    norm_time = product_time + PRODUCT_TIME
    end_time = norm_time + blocks * NORM_TIME
    moves = [
        (EARLY_PLAN[stage] + EARLY_SHIFT * (n // 2), job, stage)
        for n, job in enumerate(early)
        for stage in range(1, STAGES + 1)
    ]
    begins = []
    for job in late:
        piece = min((job.end - 1) // slab_rows, pieces)
        begins.append(piece + 1 + channel_step if piece < pieces else product_step)
        ready = channel_time + (piece + 1.3) * CHANNEL_TIME if piece < pieces else product_time + PRODUCT_TIME * 0.35
        moves += [(ready + LATE_PLAN[stage], job, stage) for stage in range(1, STAGES + 1)]
    moves.sort(key=lambda move: move[0])
    placed = []

    def advance(grid_step, since, until):
        due = [move for move in moves if since < move[0] <= until]
        placed.extend(due)
        if due:

            @pl.when(step == grid_step)
            def _():
                for _, job, stage in due:
                    job.move(stage)

    def advance_each(first, number, start, length, since, until):
        for n in range(number):
            base = start + n * length
            advance(first + n, base + since * length, base + until * length)

    @pl.when(step == 0)
    def _():
        greet(axes, ("seq", "x", "z"))
        for copy in pair_copies:
            copy.start()
        for job in early:
            job.start(0)
        for load in loads:
            load.start()
        set_spread(spread)
        for piece in range(inner // LANES):
            lanes = slice(piece * LANES, (piece + 1) * LANES)
            gather[lanes, :] = flip(spread[:, lanes])
        set_rate(heads_ref, a_log_ref)
        heads_ref[SKIP : SKIP + 1, :] = head_row(skip_in[...])
        set_conv(conv_ref, weight_ref, bias_ref)
        set_step_weight(wdt_ref, wdt_in)
        for lanes in chunks(inner):
            skip[:, lanes] = dot(
                parts(jnp.broadcast_to(heads_ref[SKIP : SKIP + 1, :], (8, LANES))), spread[:, lanes]
            )
        gconv[:, tok_rows:, :] = jnp.zeros((WIDE // LANES, 8, LANES), F32)
        for ref in (x_ginf, column, d_final, gcw, gcb, gdtb, grate, gskip, gng):
            ref[...] = jnp.zeros_like(ref)

    @pl.when(step < blocks)
    def _():
        first_half = half_mask()
        for sub in range(SUBS):
            rows = slice(sub * SUB, (sub + 1) * SUB)
            all_rows = pl.ds(pl.multiple_of(step * BLOCK + sub * SUB, SUB), SUB)
            number = step * SUBS + sub
            b_in, c_out = bc_ref[all_rows, :STATE], bc_ref[all_rows, STATE:]
            dt_low = dt_ref[all_rows, :]
            meet = jnp.where(later, dot_t(b_in, c_out), 0.0)
            run = dot(ones, dt_low) * heads_ref[RATE : RATE + 1, :]
            final = run[SUB - 1 : SUB]
            run_t = run.T
            factors[number] = jnp.concatenate(
                [dt_low, parts(jnp.exp2(final - run)), parts(jnp.exp2(run))], axis=0
            )
            finals[number] = parts(jnp.broadcast_to(jnp.exp2(final), (16, LANES)))
            c_flip[number] = flip(c_out)
            spread_dt = dot(dt_low, spread[...])
            g_meet = jnp.zeros((SUB, SUB), F32)
            for pair in range(inner // LANES):
                lanes = slice(pair * LANES, (pair + 1) * LANES)
                inflow = spread_dt[:, lanes] * x_row[rows, lanes].astype(F32)
                g_diag = pair_diag(gy_row[rows, lanes], first_half)
                g_scores = dot_t(inflow.astype(BF16), g_diag)
                scores = []
                for half, head in enumerate((2 * pair, 2 * pair + 1)):
                    decay = jnp.exp2(jnp.minimum(run_t[head : head + 1, :] - run[:, head : head + 1], 0.0))
                    scores.append((decay * meet).astype(BF16))
                    g_meet += decay * g_scores[:, half * SUB : (half + 1) * SUB]
                ginf[all_rows, lanes] = dot(jnp.concatenate(scores, axis=1), g_diag)
                if pair == inner // LANES // 2 - 1:
                    advance_each(0, blocks, 0.0, WITHIN_TIME, sub / SUBS, (sub + 0.5) / SUBS)
            g_meet = jnp.where(later, g_meet, 0.0).astype(BF16)
            g_bc[all_rows, :STATE] = dot(g_meet, c_out)
            g_bc[all_rows, STATE:] = t_dot(g_meet, b_in)
            advance_each(0, blocks, 0.0, WITHIN_TIME, (sub + 0.5) / SUBS, (sub + 1) / SUBS)

    @pl.when(step == 0)
    def _():
        for copy in pair_copies:
            copy.wait()
        mine, other = adj_ref[:, half].astype(F32), pair_adj[:, half].astype(F32)
        decay = jnp.exp2(logds_ref[2 * y, 0:1, half])
        chip_adj[...] = jnp.where(core == 0, mine + decay * other, other + decay * mine).astype(BF16)
        for copy in chip_copies:
            copy.start()

    @pl.when(step == blocks // 2)
    def _():
        for copy in chip_copies:
            copy.wait()
        for copy in half_copies:
            copy.start()

    @pl.when(step == channel_step)
    def _():
        for copy in half_copies:
            copy.wait()
        for load in loads:
            load.wait()

    def rim_copy(slot):
        return shift_copy(axes, rim_send.at[slot], rim_recv.at[slot], -1, rim_sems.at[0, slot], rim_sems.at[1, slot])

    def conv_back(slot, source, xbc, halo, at):
        for n in range(WIDE // LANES):
            lanes = slice(at + n * LANES, at + (n + 1) * LANES)
            ext[n, 0:RIM, :] = halo[:, lanes].astype(F32)
            ext[n, RIM:, :] = xbc[:, lanes].astype(F32)

        @pl.loop(0, WIDE // LANES)
        def _(n):
            lanes = tile(slot * (WIDE // LANES) + n)
            from_lanes = tile(at // LANES + n)
            taps = [conv_ref[k : k + 1, lanes] for k in range(CONV)]
            bias = conv_ref[CONV : CONV + 1, lanes]
            sums = [jnp.zeros((8, LANES), F32) for _ in range(CONV + 1)]
            for row in range(0, tok_rows, 64):
                start = row + RIM - (CONV - 1)
                shifted = [ext[n, start + k : start + k + 64, :] for k in range(CONV)]
                total = bias
                for k in range(CONV):
                    total = total + taps[k] * shifted[k]
                sig = sigmoid(total)
                g_act = source[row : row + 64, from_lanes].astype(F32)
                g_conv = g_act * (sig * (1.0 + total * (1.0 - sig)))
                gconv[n, row : row + 64, :] = g_conv
                for k in range(CONV):
                    sums[k] += fold(g_conv * shifted[k])
                sums[CONV] += fold(g_conv)
            for k in range(CONV):
                gcw[k, :, lanes] += sums[k]
            gcb[:, lanes] += sums[CONV]
            for row in range(0, tok_rows, 64):
                total = taps[CONV - 1] * gconv[n, row : row + 64, :]
                for k in range(CONV - 1):
                    start = row + CONV - 1 - k
                    total = total + taps[k] * gconv[n, start : start + 64, :]
                gx_all[row : row + 64, lanes] = total.astype(BF16)
            last[slot, :, tile(n)] = total[64 - RIM :]

        rim_send[slot] = gconv[:, 0:8, :]
        rim_copy(slot).start()

    def finish_slot(slot):
        rim_copy(slot).wait()
        row = lax.broadcasted_iota(jnp.int32, (8, LANES), 0)
        for n in range(WIDE // LANES):
            at = tile(slot * (WIDE // LANES) + n)
            rim = jnp.where(me == count - 1, jnp.zeros((8, LANES), F32), rim_recv[slot, n])
            fix = jnp.zeros((8, LANES), F32)
            for k in range(CONV - 1):
                moved = pltpu.roll(rim, 8 - CONV + 1 + k, 0)
                fix += jnp.where(row >= 8 - CONV + 1 + k, conv_ref[k : k + 1, at] * moved, 0.0)
            old = last[slot, :, n * LANES : (n + 1) * LANES]
            gx_all[tok_rows - RIM :, at] = jnp.concatenate([old[0:8], old[8:] + fix], axis=0).astype(BF16)

    def weight_gradient(piece, size):
        for m in range(features // BLOCK):
            part = dot(norm_t[m * BLOCK : (m + 1) * BLOCK, :], gx_all[:, pl.ds(pl.multiple_of(piece * PIECE, PIECE), size)])
            for n in range(size // LANES):
                at = pl.multiple_of(piece * slab_rows + n * features + m * BLOCK, 16)
                late_src[pl.ds(at, BLOCK), :] = part[:, n * LANES : (n + 1) * LANES].astype(BF16)

    def begin_late(last_piece):
        for job, begin in zip(late, begins):
            if ((job.end - 1) // slab_rows == pieces - 1) == last_piece and (job.end - 1) // slab_rows < pieces:

                @pl.when(step == begin)
                def _():
                    job.start(0)

    def finish_piece(piece, last_piece):
        for n in range(PIECE // WIDE):
            finish_slot(piece * (PIECE // WIDE) + n)
        weight_gradient(piece, PIECE)
        begin_late(last_piece)

    @pl.when((step >= channel_step) & (step < product_step))
    def _():
        piece = step - channel_step
        lanes = tile(piece, PIECE)
        spread_p = spread[:, lanes]
        gather_p = gather[lanes, :]
        skip_p = skip[0:1, lanes]
        after = jnp.zeros((STATE, PIECE), F32)
        for chip in reversed(range(y_count)):
            decay = jnp.exp2(logds_ref[2 * chip, 0:1, lanes] + logds_ref[2 * chip + 1, 0:1, lanes])
            after = jnp.where(chip > y, decay * after + chips[chip, :, lanes].astype(F32), after)
        decay = jnp.exp2(logds_ref[2 * y + 1, 0:1, lanes])
        after = jnp.where(core == 0, decay * after + pair_adj[:, lanes].astype(F32), after)
        skipped = [jnp.zeros((8, LANES), F32) for _ in range(PIECE // LANES)]
        for sub in reversed(range(subs)):
            rows = slice(sub * SUB, (sub + 1) * SUB)
            wide = dot(jnp.concatenate([factors[sub], finals[sub]], axis=0), spread_p)
            dt_e, to_end, from_start = wide[:SUB], wide[SUB : 2 * SUB], wide[2 * SUB : 3 * SUB]
            kept = wide[3 * SUB : 3 * SUB + 1]
            after_low = after.astype(BF16)
            start_low = starts_ref[sub]
            from_b = dot(bc_ref[rows, :STATE], after_low)
            operands = [[], [], [], [], []]
            block_sums = []
            for n in range(PIECE // LANES):
                at = slice(n * LANES, (n + 1) * LANES)
                columns = [[], [], [], [], []]
                block_sum = jnp.zeros((8, LANES), F32)
                skip_sum = jnp.zeros((8, LANES), F32)
                for row in range(0, SUB, 32):
                    here = slice(row, row + 32)
                    there = slice(sub * SUB + row, sub * SUB + row + 32)
                    x = x_col[there, at].astype(F32)
                    g_y = gy_col[there, at].astype(F32)
                    inflow = dt_e[here, at] * x
                    inflow_low = inflow.astype(BF16).astype(F32)
                    from_after = to_end[here, at] * from_b[here, at]
                    g_inflow = ginf[there, tile(piece * (PIECE // LANES) + n)] + from_after
                    act[there, at] = (dt_e[here, at] * g_inflow + skip_p[:, at] * g_y).astype(BF16)
                    product = inflow_low * g_inflow
                    high = product.astype(BF16)
                    columns[0].append((x * g_inflow).astype(BF16))
                    columns[1].append(high)
                    columns[2].append((product - high.astype(F32)).astype(BF16))
                    columns[3].append((from_start[here, at] * g_y).astype(BF16))
                    columns[4].append((to_end[here, at] * inflow).astype(BF16))
                    block_sum += fold(inflow_low * from_after)
                    skip_sum += fold(g_y * x)
                for operand, column_parts in zip(operands, columns):
                    operand.append(jnp.concatenate(column_parts, axis=0))
                block_sums.append(block_sum)
                skipped[n] += skip_sum
            x_g, high, low, scaled, weighted = [jnp.concatenate(operand, axis=1) for operand in operands]
            block_sum = jnp.concatenate(block_sums, axis=1) + kept * fold(
                start_low.astype(F32) * after_low.astype(F32)
            )
            sum_high = block_sum.astype(BF16).astype(F32)
            both = jnp.concatenate([sum_high, block_sum - sum_high], axis=0).astype(BF16)
            head_sums = dot(jnp.concatenate([x_g, high, low, both], axis=0), gather_p)
            x_ginf[rows, :] += head_sums[:SUB]
            column[rows, :] += head_sums[SUB : 2 * SUB] + head_sums[2 * SUB : 3 * SUB]
            d_final[sub] += head_sums[3 * SUB : 3 * SUB + 8] + head_sums[3 * SUB + 8 :]
            g_bc[rows, :STATE] += dot_t(weighted, after_low)
            g_bc[rows, STATE:] += dot_t(scaled, start_low)
            after = kept * after + dot(c_flip[sub], scaled)
            if sub == subs - 3:

                @pl.when(step > channel_step)
                def _():
                    finish_piece(piece - 1, False)

            done = (subs - sub) / subs * 0.7
            advance_each(channel_step, pieces, channel_time, CHANNEL_TIME, done - 0.7 / subs, done)
        gskip[:, lanes] += jnp.concatenate(skipped, axis=1)
        for n in range(PIECE // WIDE):
            conv_back(piece * (PIECE // WIDE) + n, act, xbc_ref, xhalo_ref, n * WIDE)
            since = 0.7 + 0.3 * n / (PIECE // WIDE)
            advance_each(
                channel_step, pieces, channel_time, CHANNEL_TIME, since, since + 0.3 / (PIECE // WIDE) + 1e-6
            )

    @pl.when(step == product_step)
    def _():
        conv_back(inner // WIDE, g_bc, xbc_rest, xhalo_rest, 0)
        finish_piece(pieces - 1, True)
        upper = jnp.where(later, 1.0, 0.0).astype(BF16)
        rate = heads_ref[RATE : RATE + 1, :] * (1.0 / LOG2E)
        rest = jnp.concatenate(
            [rowdot_ref[sub * SUB : (sub + 1) * SUB, :] - column[sub * SUB : (sub + 1) * SUB, :] for sub in range(subs)],
            axis=1,
        )
        sums = jnp.zeros_like(rest)
        for _ in range(3):
            part = rest.astype(BF16)
            sums += dot(upper, part)
            rest = rest - part.astype(F32)
        for sub in range(subs):
            rows = slice(sub * SUB, (sub + 1) * SUB)
            dt_f = dt_ref[rows, :].astype(F32)
            d_log = sums[:, sub * LANES : (sub + 1) * LANES]
            d_log = d_log + jnp.sum(d_final[sub], axis=0, keepdims=True)
            g_dt = (x_ginf[rows, :] + rate * d_log).astype(BF16).astype(F32)
            g_pre = g_dt * sig_ref[rows, :]
            gdt_all[rows, :] = g_pre.astype(BF16)
            gdtb[...] += fold(g_pre)
            grate[...] += fold(dt_f * d_log)
        advance(product_step, product_time, product_time + 0.2 * PRODUCT_TIME)
        finish_slot(inner // WIDE)
        weight_gradient(pieces, WIDE)
        at = width // LANES * features
        pack_slabs(late_src, at, 32, 0, dot_t(flip(gdt_all[...])[:32], norm_t[...]))
        used = at + 32 * features // LANES
        if late_src.shape[0] > used:
            late_src[used:, :] = jnp.zeros((late_src.shape[0] - used, LANES), BF16)
        for job in late:
            if (job.end - 1) // slab_rows >= pieces:
                job.start(0)
        for m in range(blocks):
            rows = slice(m * BLOCK, (m + 1) * BLOCK)
            gn[rows, :] = (
                dot_t(gz_ref[rows, :], wz_ref[...])
                + dot_t(gx_all[rows, :], wx_ref[...])
                + dot(gdt_all[rows, :], wdt_ref[...])
            )
            since = 0.2 if m == 0 else 0.4 + 0.6 * m / blocks
            until = 0.4 + 0.6 * (m + 1) / blocks
            advance(
                product_step, product_time + since * PRODUCT_TIME,
                product_time + until * PRODUCT_TIME if m < blocks - 1 else norm_time,
            )

    @pl.when(step >= norm_step)
    def _():
        block = step - norm_step
        rows = tile(block, BLOCK)
        g_normed = gn[rows, :]
        residual, rms = norm_rows(tok_ref[0])
        unit = residual * rms
        gng[...] += fold(g_normed * unit)
        h = g_normed * gain_ref[...].reshape(1, -1)
        pull = jnp.sum(h * unit, axis=-1, keepdims=True) * (1.0 / features)
        grad_ref[0] = (cot_ref[0].astype(F32) + rms * (h - unit * pull)).astype(BF16)
        advance_each(norm_step, blocks, norm_time, NORM_TIME, 0.0, 1.0)

    @pl.when(step == norm_step + blocks - 1)
    def _():
        starts, _ = vector_rows(features, width, inner)

        def put(row, ref):
            value = ref if ref.shape[0] == 1 else jnp.sum(ref, axis=0, keepdims=True)
            for n in range(value.shape[1] // LANES):
                vec[row + n : row + n + 1, :] = value[:, n * LANES : (n + 1) * LANES]

        vec[...] = jnp.zeros_like(vec)
        put(starts[0], gng[...])
        for k in range(CONV):
            put(starts[1] + k * width // LANES, gcw[k])
        put(starts[2], gcb[...])
        put(starts[3], ggain_ref[...])
        put(starts[4], gdtb[...])
        put(starts[5], grate[...] * (heads_ref[RATE : RATE + 1, :] * (1.0 / LOG2E)))
        put(starts[6], split_dot_t(gskip[...], spread[...]))
        vector.start(0)
        rest = [move for move in moves if move[0] > end_time]
        assert len(placed) + len(rest) == len(moves)
        for n, (_, job, stage) in enumerate(rest):
            job.move(stage)
            level, turn = divmod(n + 1, max(1, len(rest) // 5))
            if turn == 0 and level <= 4:
                vector.finish(level - 1)
                if level < 4:
                    vector.start(level)
        vec_out[...] = vec[...]


WITHIN_TIME = 5.0
CHANNEL_TIME = 12.0
PRODUCT_TIME = 14.0
NORM_TIME = 1.2
EARLY_PLAN = (0, 6, 17, 25, 36, 46, 54, 65, 71)
EARLY_SHIFT = 8
LATE_PLAN = (0, 4, 9, 13, 18, 23, 27, 32, 36)


def unpack_kernel(
    wo_ref, wz_ref, wx_ref, wdt_ref, vec_ref, out_in, grad_in,
    out_ref, grad_ref, gwo_ref, gwz_ref, gwx_ref, gwdt_ref, gng_ref, gcw_ref, gcb_ref, gdtb_ref, ga_ref, gskip_ref, ggain_ref,
):
    def slabs(source, target):
        rows = target.shape[0]
        for n in range(target.shape[1] // LANES):
            target[:, n * LANES : (n + 1) * LANES] = source[n * rows : (n + 1) * rows, :].astype(F32)

    out_ref[...] = out_in[...]
    grad_ref[...] = grad_in[...]
    slabs(wo_ref, gwo_ref)
    slabs(wz_ref, gwz_ref)
    slabs(wx_ref, gwx_ref)

    @pl.when(pl.program_id(0) == 0)
    def _():
        heads, features = gwdt_ref.shape
        width = gcb_ref.shape[0]
        at, _ = vector_rows(features, width, ggain_ref.shape[0])
        for n in range(features // LANES):
            gwdt_ref[:, n * LANES : (n + 1) * LANES] = wdt_ref[n * 32 : n * 32 + heads, :].astype(F32)

        def rows(start, size):
            return jnp.concatenate([vec_ref[start + n : start + n + 1, :] for n in range(size // LANES)], axis=1)

        gng_ref[...] = rows(at[0], features).reshape(-1)
        for k in range(CONV):
            gcw_ref[k : k + 1, :] = rows(at[1] + k * width // LANES, width)
        gcb_ref[...] = rows(at[2], width).reshape(-1)
        ggain_ref[...] = rows(at[3], ggain_ref.shape[0]).reshape(-1)
        for n, ref in enumerate((gdtb_ref, ga_ref, gskip_ref)):
            ref[...] = vec_ref[at[4 + n] : at[4 + n] + 1, :][0, :heads]


def unpack(early, late, vec, out, grad, inner, width, features, heads):
    sds = jax.ShapeDtypeStruct
    grid = width // WIDE
    last = inner // WIDE - 1
    first = inner * features // LANES // (2 * features)
    stop = width // LANES * features
    rest = 32 * features // LANES
    passed = pl.BlockSpec((1, BLOCK, features), lambda i: (0, jnp.minimum(i, out.shape[1] // BLOCK - 1), 0))
    vectors = [(heads, features), (features,), (CONV, width), (width,), (heads,), (heads,), (heads,), (inner,)]
    return pl.pallas_call(
        unpack_kernel,
        grid=(grid,),
        in_specs=[
            pl.BlockSpec((inner, LANES), lambda i: (jnp.minimum(i, features // LANES - 1), 0)),
            pl.BlockSpec((2 * features, LANES), lambda i: (first + jnp.minimum(i, last), 0)),
            pl.BlockSpec((2 * features, LANES), lambda i: (i, 0)),
            pl.BlockSpec((rest, LANES), lambda i: (stop // rest, 0)),
            whole(vec.shape), passed, passed,
        ],
        out_specs=[
            passed, passed,
            pl.BlockSpec((inner, LANES), lambda i: (0, jnp.minimum(i, features // LANES - 1))),
            pl.BlockSpec((features, WIDE), lambda i: (0, jnp.minimum(i, last))),
            pl.BlockSpec((features, WIDE), lambda i: (0, i)),
            *[whole(shape) for shape in vectors],
        ],
        out_shape=[
            sds(out.shape, BF16), sds(grad.shape, BF16),
            sds((inner, features), F32), sds((features, inner), F32), sds((features, width), F32),
            *[sds(shape, F32) for shape in vectors],
        ],
        compiler_params=pltpu.CompilerParams(vmem_limit_bytes=VMEM_LIMIT),
        name="unpack",
    )(early, early, late, late, vec, out, grad)


def whole(shape):
    return pl.BlockSpec(shape, lambda i: (0,) * len(shape), pipeline_mode=pl.Buffered(1))


def params(collective_id):
    return pltpu.CompilerParams(
        vmem_limit_bytes=VMEM_LIMIT, dimension_semantics=("arbitrary",), collective_id=collective_id, has_side_effects=True
    )


def local(
    tokens, lengths, cotangent, norm_gain, w_z, w_xbc, w_dt, conv_weight, conv_bias, dt_bias, a_log, d_skip, gate_gain, w_out
):
    tok_rows, features = tokens.shape[1:]
    inner = w_z.shape[1]
    width = w_xbc.shape[1]
    heads = a_log.shape[0]
    steps = tok_rows // BLOCK
    seq_count = lax.axis_size("seq")
    devices = lax.axis_size("dp") * seq_count
    sds = jax.ShapeDtypeStruct
    dma = pltpu.SemaphoreType.DMA

    head_scratch = [pltpu.VMEM((8, LANES), F32)]

    def rows3(n, at, single=False):
        return pl.BlockSpec((1, BLOCK, n), lambda i: (0, at(i), 0), pipeline_mode=pl.Buffered(1 if single else 2))

    def rows2(n, at, single=False):
        return pl.BlockSpec((BLOCK, n), lambda i: (at(i), 0), pipeline_mode=pl.Buffered(1 if single else 2))

    def tail_at(block):
        return jnp.maximum(block * (BLOCK // RIM) - 1, 0)

    def back(i):
        return steps - 1 - i

    normed, xbc, x, bc, dt, sig, added, state, logd, xbc_halo = pl.pallas_call(
        enter_kernel,
        grid=(steps,),
        in_specs=[
            rows3(features, back),
            pl.BlockSpec((1, RIM, features), lambda i: (0, tail_at(back(i)), 0)),
            pl.BlockSpec((1, RIM, features), lambda i: (0, tok_rows // RIM - 1, 0), pipeline_mode=pl.Buffered(1)),
            whole((features,)), whole((features, width)), whole((heads, features)), whole((CONV, width)), whole((width,)),
            whole((heads,)), whole((heads,)),
        ],
        out_specs=[
            rows2(features, back), rows2(width, back), rows2(inner, back), rows2(2 * STATE, back), rows2(LANES, back),
            rows2(LANES, back), pl.BlockSpec((SUBS, STATE, inner), lambda i: (back(i), 0, 0)),
            whole((STATE, inner)), whole((8, inner)), whole((RIM, width)),
        ],
        out_shape=[
            sds((tok_rows, features), BF16), sds((tok_rows, width), BF16), sds((tok_rows, inner), BF16),
            sds((tok_rows, 2 * STATE), BF16), sds((tok_rows, LANES), BF16), sds((tok_rows, LANES), F32),
            sds((tok_rows // SUB, STATE, inner), BF16), sds((STATE, inner), BF16), sds((8, inner), F32),
            sds((RIM, width), BF16),
        ],
        scratch_shapes=[
            pltpu.VMEM((BLOCK + RIM, width), F32),
            pltpu.VMEM((LANES, inner), BF16), pltpu.VMEM((width // LANES, BLOCK + RIM, LANES), F32),
            pltpu.VMEM((STATE, inner), F32), pltpu.VMEM((8, inner), F32), pltpu.VMEM((RIM, features), BF16),
            pltpu.VMEM((RIM, features), BF16), pltpu.VMEM((RIM, width), BF16), pltpu.VMEM((RIM, width), BF16), *head_scratch, pltpu.VMEM((8, width), F32),
            pltpu.VMEM((LANES, features), BF16), dma, dma, dma((2,)),
        ],
        compiler_params=params(0),
        name="enter",
    )(tokens, tokens, tokens, norm_gain, w_xbc, w_dt.T, conv_weight, conv_bias, dt_bias, a_log)

    count = seq_count - 1
    early_rows = padded(2 * inner * features // LANES, 16 * devices)
    late_rows = padded((width + 32) * features // LANES, 16 * devices)

    def either(i):
        return lax.rem(i, steps)

    def second(i):
        return jnp.maximum(i - steps, 0)

    out, g_y, g_z, starts, rowdot, adj, early, g_gain, logds, norm_t = pl.pallas_call(
        middle_kernel,
        grid=(2 * steps,),
        in_specs=[
            pl.BlockSpec(memory_space=pltpu.SMEM),
            rows3(features, second), rows3(features, either), rows2(features, either), rows2(inner, either),
            rows2(2 * STATE, either), rows2(LANES, either),
            pl.BlockSpec((SUBS, STATE, inner), lambda i: (second(i), 0, 0)), whole((STATE, inner)), whole((8, inner)),
            whole((features, inner)), whole((inner, features)), whole((inner,)), whole((heads,)), whole((heads,)),
        ],
        out_specs=[
            rows3(features, second), rows2(inner, second), rows2(inner, second),
            pl.BlockSpec((SUBS, STATE, inner), lambda i: (second(i), 0, 0)),
            rows2(LANES, second), whole((STATE, inner)), whole((early_rows, LANES)), whole((8, inner)),
            whole((seq_count, 8, inner)), whole((features, tok_rows)),
        ],
        out_shape=[
            sds((1, tok_rows, features), BF16), sds((tok_rows, inner), BF16), sds((tok_rows, inner), BF16),
            sds((tok_rows // SUB, STATE, inner), BF16), sds((tok_rows, LANES), F32),
            sds((STATE, inner), BF16), sds((early_rows, LANES), BF16), sds((8, inner), F32),
            sds((seq_count, 8, inner), F32), sds((features, tok_rows), BF16),
        ],
        scratch_shapes=[
            pltpu.VMEM((SUB + 16, inner), F32),
            pltpu.VMEM((LANES, inner), BF16), pltpu.VMEM((steps, BLOCK, inner), F32), pltpu.VMEM((STATE, inner), F32),
            pltpu.VMEM((8, LANES), F32), pltpu.VMEM((8, inner), F32), pltpu.VMEM((tok_rows, inner), F32),
            pltpu.VMEM((tok_rows, inner), F32), pltpu.VMEM((tok_rows, inner), BF16), pltpu.VMEM((tok_rows, inner), BF16),
            pltpu.VMEM((tok_rows, features), BF16), pltpu.VMEM((features, tok_rows), BF16),
            pltpu.VMEM((STATE, inner), F32), pltpu.VMEM((8, inner), F32),
            pltpu.VMEM((STATE, inner), BF16), pltpu.VMEM((STATE, inner // 2), BF16),
            pltpu.VMEM((seq_count // 2, STATE, inner), BF16), pltpu.VMEM((seq_count, 8, inner), F32),
            *head_scratch, pltpu.VMEM((8, inner), F32), dma((seq_count,)), dma((seq_count,)), dma((count,)), dma((count,)),
        ],
        compiler_params=params(1),
        name="middle",
    )(lengths, tokens, cotangent, normed, x, bc, dt, added, state, logd, w_z, w_out, gate_gain, a_log, d_skip)

    pieces = inner // PIECE
    norm_step = steps + pieces + 1

    def first(i):
        return jnp.minimum(i, steps - 1)

    def column(rows, most):
        return pl.BlockSpec((rows, PIECE), lambda i: (0, jnp.clip(i - steps, 0, most)))

    def rest(rows):
        return pl.BlockSpec((rows, WIDE), lambda i: (0, inner // WIDE), pipeline_mode=pl.Buffered(1))

    def final(i):
        return jnp.clip(i - norm_step, 0, steps - 1)

    _, vec_rows = vector_rows(features, width, inner)
    sizes = axis_sizes()
    reach = max(sizes) - 1
    tiles = WIDE // LANES
    grad, early, late, vec = pl.pallas_call(
        back_kernel,
        grid=(norm_step + steps,),
        in_specs=[
            rows2(inner, first, True), column(tok_rows, pieces - 1), rows2(inner, first, True), column(tok_rows, pieces - 1),
            whole((tok_rows, 2 * STATE)), whole((tok_rows, LANES)), whole((tok_rows, LANES)), whole((tok_rows, LANES)),
            pl.BlockSpec((tok_rows // SUB, STATE, PIECE), lambda i: (0, 0, jnp.clip(i - steps, 0, pieces - 1))),
            column(tok_rows, pieces - 1), column(RIM, pieces - 1), rest(tok_rows), rest(RIM),
            whole((STATE, inner)), whole((seq_count, 8, inner)), whole((early_rows, LANES)), whole((8, inner)),
            rows3(features, final, True), rows3(features, final, True), *[pl.BlockSpec(memory_space=pl.ANY)] * 4,
            whole((heads, features)), whole((features,)),
            whole((CONV, width)), whole((width,)), whole((heads,)), whole((heads,)),
        ],
        out_specs=[
            rows3(features, final), pl.BlockSpec(memory_space=pl.ANY), pl.BlockSpec(memory_space=pl.ANY),
            whole((vec_rows, LANES)),
        ],
        out_shape=[
            sds((1, tok_rows, features), BF16), sds((early_rows, LANES), BF16), sds((late_rows, LANES), BF16),
            sds((vec_rows, LANES), F32),
        ],
        scratch_shapes=[
            pltpu.VMEM((LANES, inner), BF16), pltpu.VMEM((inner, LANES), BF16), pltpu.VMEM((tok_rows, inner), F32),
            pltpu.VMEM((tok_rows // SUB, 3 * SUB, LANES), BF16), pltpu.VMEM((tok_rows // SUB, 16, LANES), BF16),
            pltpu.VMEM((tok_rows // SUB, STATE, SUB), BF16), pltpu.VMEM((tok_rows, 2 * STATE), F32),
            pltpu.VMEM((tok_rows, LANES), F32), pltpu.VMEM((tok_rows, LANES), F32),
            pltpu.VMEM((tok_rows // SUB, 8, LANES), F32), pltpu.VMEM((8, inner), F32),
            pltpu.VMEM((tok_rows, PIECE), BF16), pltpu.VMEM((tiles, tok_rows + RIM, LANES), F32),
            pltpu.VMEM((tiles, tok_rows + 8, LANES), F32), pltpu.VMEM((tok_rows, width), BF16),
            pltpu.VMEM((tok_rows, LANES), BF16), pltpu.VMEM((width // WIDE, RIM, WIDE), F32),
            pltpu.VMEM((width // WIDE, tiles, 8, LANES), F32), pltpu.VMEM((width // WIDE, tiles, 8, LANES), F32),
            pltpu.VMEM((CONV, 8, width), F32), pltpu.VMEM((8, width), F32), pltpu.VMEM((8, LANES), F32),
            pltpu.VMEM((8, LANES), F32), pltpu.VMEM((8, inner), F32), pltpu.VMEM((8, features), F32),
            pltpu.VMEM((STATE, inner), BF16), pltpu.VMEM((STATE, inner // 2), BF16),
            pltpu.VMEM((seq_count // 2, STATE, inner), BF16), pltpu.VMEM((early_rows, LANES), BF16),
            pltpu.VMEM((late_rows, LANES), BF16), pltpu.VMEM((late_rows, LANES), BF16),
            pltpu.VMEM((vec_rows, LANES), F32), pltpu.VMEM((sum(sizes), vec_rows, LANES), F32),
            *head_scratch, pltpu.VMEM((8, width), F32), pltpu.VMEM((LANES, features), BF16),
            pltpu.VMEM((features, tok_rows), BF16), pltpu.VMEM((tok_rows, inner), BF16),
            pltpu.VMEM((features, inner), BF16), pltpu.VMEM((features, width), BF16),
            dma((2, MOST_JOBS, STAGES, reach)), dma((2, MOST_JOBS, STAGES, reach)), dma((2, MOST_JOBS)),
            dma((2, 4, reach)), dma((seq_count,)), dma((seq_count,)), dma((2, width // WIDE)), dma((4,)),
        ],
        compiler_params=params(2),
        name="back",
    )(
        x, x, g_y, g_y, bc, dt, sig, rowdot, starts, xbc, xbc_halo, xbc, xbc_halo, adj, logds, early, g_gain,
        tokens, cotangent, norm_t, g_z, w_z, w_xbc, w_dt.T, norm_gain, conv_weight, conv_bias, a_log, d_skip,
    )

    out, grad, g_wo, g_wz, g_wx, g_wdt, g_ng, g_cw, g_cb, g_dtb, g_a, g_skip, g_gain = unpack(
        early, late, vec, out, grad, inner, width, features, heads
    )
    return out, grad, g_ng, g_wz, g_wx, g_wdt.T, g_cw, g_cb, g_dtb, g_a, g_skip, g_gain, g_wo


def solution(mesh):
    rows = P("dp", "seq", None)
    return jax.shard_map(
        local,
        mesh=mesh,
        in_specs=(rows, P("dp"), rows) + (P(),) * 11,
        out_specs=(rows, rows) + (P(),) * 11,
        check_vma=False,
    )
```

time: 1050 us -> 209 us (0.20); the launches traced: 1040 us -> 209 us
  waiting for transfers between devices: 272 us -> 0 us
  local copies, waits for them, and re-layouts: 241 us -> 0 us
  matrix products: 234 us -> 0 us
  Pallas kernels: 0 us -> 207 us
  other arithmetic: 198 us -> 0 us
  blocking collectives: 43.5 us -> 0 us
  starting transfers between devices: 32.8 us -> 0 us
  between operations: 15.7 us -> 1.49 us
    dot_general x26 -> x0, matrix products: 234 us -> none  [the longest x3 77.1 us: state_scan(): within = jnp.einsum('chts,cshp->cthp', scores, inflow, precision=HIGH)]
    pallas_call x0 -> x4, Pallas kernels: none -> 207 us  [the longest x1 126 us: local(): pl.pallas_call(back_kernel, grid=(norm_step + steps,), in_specs=[rows2(in...]
    psum x1 -> x0, waiting for transfers between devices: 186 us -> none  [local(): lax.psum((grad_norm_gain, grad_w_z, grad_w_xbc, grad_w_dt, grad_conv_weig...]
    convert_element_type x17 -> x0, local copies, waits for them, and re-layouts: 95.8 us -> none  [the longest x3 24 us: local(): y_float = y_tokens.reshape(tok_rows, INNER).astype(jnp.float32)]
    all_to_all x6 -> x0, waiting for transfers between devices: 85.1 us -> none  [the longest x1 35.7 us: local(): lax.all_to_all(y_heads, 'seq', split_axis=0, concat_axis=1, tiled=True)]
    unnamed x142 -> x0, local copies, waits for them, and re-layouts: 50.9 us -> none
    reduce_sum x22 -> x0, other arithmetic: 45.4 us -> none  [the longest x1 20.3 us: mixer_inputs(): conv_weight[offset][None, :] * extended[offset:offset + tok_rows]]
    psum x1 -> x0, blocking collectives: 43.5 us -> none  [local(): lax.psum((grad_norm_gain, grad_w_z, grad_w_xbc, grad_w_dt, grad_conv_weig...]
  transfers between devices with their start and end apart: 11 -> 0, of which waited for: 5 -> 0; matrix products, arithmetic and copies ran while one was open for 26% -> 0% of each run, Pallas kernels for 0% -> 0%
where the time goes in v1:
time: 209 us
  Pallas kernels  207 us (99%)
    pallas_call x1, Pallas kernels, local(): pl.pallas_call(back_kernel, grid=(norm_step + steps,), in_specs=[rows2(in...  126 us
    pallas_call x1, Pallas kernels, local(): pl.pallas_call(middle_kernel, grid=(2 * steps,), in_specs=[pl.BlockSpec(m...  48.9 us
    pallas_call x1, Pallas kernels, local(): pl.pallas_call(enter_kernel, grid=(steps,), in_specs=[rows3(features, bac...  21.2 us
    pallas_call x1, Pallas kernels, unpack(): pl.pallas_call(unpack_kernel, grid=(grid,), in_specs=[pl.BlockSpec((inner...  11.1 us

profile of v1, /device:TPU:0, one launch (start us, length us, event | category | flops | bytes accessed | tf_op | source)
XLA Modules:
  0.0 208.7 jit_solution(5741450503428488059)
XLA Ops:
  1.3 21.2 %enter.1 = (bf16[1024,768]{1,0:T(8,128)(2,1)}, bf16[1024,1792]{1,0:T(8,128)(2,1)}, bf16[1024,1536]{1,0:T(8,128)(2,1)}, bf16[1024,256]{1,0:T(8,128)(2,1)}, bf16[1...) custom-call(bf16[1,1024,768]{2,1,0:T(8,128)(2,1)} %tok_ref.5, ...), custom_call_target="tpu_custom_call" | custom-call | tf_op jit(solution)/shard_map/enter/pallas_call | solution.py:1220
  22.5 48.9 %middle.1 = (bf16[1,1024,768]{2,1,0:T(8,128)(2,1)}, bf16[1024,1536]{1,0:T(8,128)(2,1)}, bf16[1024,1536]{1,0:T(8,128)(2,1)}, bf16[8,128,1536]{2,1,0:T(8,128)(2,1)...) custom-call(s32[1]{0:T(128)S(6)} %copy.27.len_ref, ...), custom_call_target="tpu_custom_call" | custom-call | tf_op jit(solution)/shard_map/middle/pallas_call | solution.py:1262
  71.4 125.9 %back.1 = (bf16[1,1024,768]{2,1,0:T(8,128)(2,1)}, bf16[18432,128]{1,0:T(8,128)(2,1)}, bf16[11264,128]{1,0:T(8,128)(2,1)}, f32[96,128]{1,0:T(8,128)}) custom-call(bf16[1024,1536]{1,0:T(8,128)(2,1)} %get-tuple-element.50.x_ref.x_row.x_col, bf16[1024,1536]{1,0:T(8,128)(2,1)} %get-tuple-element.50.x_ref.x_row.x_col, ...), custom_call_target="tpu_custom_call" | custom-call | tf_op jit(solution)/shard_map/back/pallas_call | solution.py:1318
  197.4 11.1 %unpack.1 = (bf16[1,1024,768]{2,1,0:T(8,128)(2,1)}, bf16[1,1024,768]{2,1,0:T(8,128)(2,1)}, f32[1536,768]{1,0:T(8,128)}, f32[768,1536]{1,0:T(8,128)}, f32[768,179...) custom-call(bf16[18432,128]{1,0:T(8,128)(2,1)} %get-tuple-element.69, ...), custom_call_target="tpu_custom_call" | custom-call | tf_op jit(solution)/shard_map/unpack/pallas_call | solution.py:1156

commit v2 on v1

--- a/solution.py
+++ b/solution.py
@@ -611,7 +611,7 @@
             state[...] = wide[SUB : SUB + 1, :] * state[...] + added_ref[sub].astype(F32)
         base = pl.multiple_of(block * BLOCK, BLOCK)
 
-        @pl.loop(0, BLOCK // 32)
+        @pl.loop(0, BLOCK // 32, unroll=2)
         def _(chunk):
             rows = tile(chunk, 32)
             all_rows = pl.ds(pl.multiple_of(base + chunk * 32, 32), 32)
@@ -1104,7 +1104,7 @@
 CHANNEL_TIME = 12.0
 PRODUCT_TIME = 14.0
 NORM_TIME = 1.2
-EARLY_PLAN = (0, 6, 17, 25, 36, 46, 54, 65, 71)
+EARLY_PLAN = (0, 7, 19, 28, 40, 51, 60, 72, 79)
 EARLY_SHIFT = 8
 LATE_PLAN = (0, 4, 9, 13, 18, 23, 27, 32, 36)
 

time: 209 us -> 209 us (level)
  no operation moved by 1% of the time
where the time goes in v2:
time: 209 us; the launch traced here: 208 us
  Pallas kernels  207 us (99%)
    pallas_call x1, Pallas kernels, local(): pl.pallas_call(back_kernel, grid=(norm_step + steps,), in_specs=[rows2(in...  126 us
    pallas_call x1, Pallas kernels, local(): pl.pallas_call(middle_kernel, grid=(2 * steps,), in_specs=[pl.BlockSpec(m...  48.8 us
    pallas_call x1, Pallas kernels, local(): pl.pallas_call(enter_kernel, grid=(steps,), in_specs=[rows3(features, bac...  21.2 us
    pallas_call x1, Pallas kernels, unpack(): pl.pallas_call(unpack_kernel, grid=(grid,), in_specs=[pl.BlockSpec((inner...  11.1 us

profile of v2, /device:TPU:0, one launch (start us, length us, event | category | flops | bytes accessed | tf_op | source)
XLA Modules:
  0.0 208.4 jit_solution(8248208676882899519)
XLA Ops:
  1.3 21.2 %enter.1 = (bf16[1024,768]{1,0:T(8,128)(2,1)}, bf16[1024,1792]{1,0:T(8,128)(2,1)}, bf16[1024,1536]{1,0:T(8,128)(2,1)}, bf16[1024,256]{1,0:T(8,128)(2,1)}, bf16[1...) custom-call(bf16[1,1024,768]{2,1,0:T(8,128)(2,1)} %tok_ref.5, ...), custom_call_target="tpu_custom_call" | custom-call | tf_op jit(solution)/shard_map/enter/pallas_call | solution.py:1220
  22.5 48.8 %middle.1 = (bf16[1,1024,768]{2,1,0:T(8,128)(2,1)}, bf16[1024,1536]{1,0:T(8,128)(2,1)}, bf16[1024,1536]{1,0:T(8,128)(2,1)}, bf16[8,128,1536]{2,1,0:T(8,128)(2,1)...) custom-call(s32[1]{0:T(128)S(6)} %copy.27.len_ref, ...), custom_call_target="tpu_custom_call" | custom-call | tf_op jit(solution)/shard_map/middle/pallas_call | solution.py:1262
  71.3 125.7 %back.1 = (bf16[1,1024,768]{2,1,0:T(8,128)(2,1)}, bf16[18432,128]{1,0:T(8,128)(2,1)}, bf16[11264,128]{1,0:T(8,128)(2,1)}, f32[96,128]{1,0:T(8,128)}) custom-call(bf16[1024,1536]{1,0:T(8,128)(2,1)} %get-tuple-element.50.x_ref.x_row.x_col, bf16[1024,1536]{1,0:T(8,128)(2,1)} %get-tuple-element.50.x_ref.x_row.x_col, ...), custom_call_target="tpu_custom_call" | custom-call | tf_op jit(solution)/shard_map/back/pallas_call | solution.py:1318
  197.1 11.1 %unpack.1 = (bf16[1,1024,768]{2,1,0:T(8,128)(2,1)}, bf16[1,1024,768]{2,1,0:T(8,128)(2,1)}, f32[1536,768]{1,0:T(8,128)}, f32[768,1536]{1,0:T(8,128)}, f32[768,179...) custom-call(bf16[18432,128]{1,0:T(8,128)(2,1)} %get-tuple-element.69, ...), custom_call_target="tpu_custom_call" | custom-call | tf_op jit(solution)/shard_map/unpack/pallas_call | solution.py:1156
